TPU v7x, 32 devices: a whole 2x2x4 slice. The times are simulated.
32 devices in a mesh: rows: 8 (over y, x, core), cols: 4 (over z).
Axes of the slice: x: 2, y: 2, z: 4, core: 2. Of those that a mesh axis runs over, the one named last changes fastest.
Arguments:
- tokens: bfloat16 [104, 2048], P(None, 'rows'), may hold values from -24 to 24
- arrival: int32 [104], replicated, may hold values from 0 to 103, each once
- cache_lengths: int32 [104], replicated, may hold values from 1 to 1023, as said below
- move_slot: int32 [8, 4], replicated, may hold values from 0 to 12, as said below
- move_target: int32 [8, 4], replicated, may hold values from 0 to 7, as said below
- page_table: int32 [8, 4, 13, 8], P('rows', 'cols'), may hold values from 0 to 103, as said below
- kv_pool: bfloat16 [832, 4, 32, 512], P('rows', 'cols'), may hold values from -400 to 400
- ssm_state: bfloat16 [104, 32, 64, 256], P('rows', 'cols'), may hold values from -1.5 to 1.5
- conv_x: bfloat16 [104, 3, 2048], P('rows', None, 'cols'), may hold values from -6 to 6
- conv_bc: bfloat16 [104, 3, 512], P('rows'), may hold values from -6 to 6
- norm_gain: bfloat16 [2048], P('rows'), may hold values from 0.099609375 to 1.8984375
- weight_z: bfloat16 [2048, 2048], P('rows', 'cols'), may hold values from -0.125 to 0.125
- weight_x: bfloat16 [2048, 2048], P('rows', 'cols'), may hold values from -0.125 to 0.125
- weight_dt: bfloat16 [2048, 32], P('rows', 'cols'), may hold values from -0.125 to 0.125
- weight_bc: bfloat16 [2048, 512], P('rows'), may hold values from -0.125 to 0.125
- weight_qkv: bfloat16 [2048, 1536], P('rows'), may hold values from -0.125 to 0.125
- conv_weight_x: bfloat16 [4, 2048], P(None, 'cols'), may hold values from -3 to 3
- conv_weight_bc: bfloat16 [4, 512], replicated, may hold values from -3 to 3
- dt_bias: float32 [32], P('cols'), may hold values from -4 to -1
- a_log: float32 [32], P('cols'), may hold values from 0 to 2.5
- d_skip: float32 [32], P('cols'), may hold values from 0.5 to 1.5
- weight_ssm_out: bfloat16 [2048, 2048], P('cols'), may hold values from -0.125 to 0.125
- weight_attn_out: bfloat16 [1024, 2048], P('cols'), may hold values from -0.1875 to 0.1875
Outputs:
- mixed: bfloat16 [104, 2048], P('rows', 'cols')
- ssm_next: bfloat16 [104, 32, 64, 256], P('rows', 'cols')
- conv_x_next: bfloat16 [104, 3, 2048], P('rows', None, 'cols')
- conv_bc_next: bfloat16 [104, 3, 512], P('rows')
- kv_next: bfloat16 [832, 4, 32, 512], P('rows', 'cols')
Inputs may be any that keep to these rules, and one draw needn't show every extreme that they name: `cache_lengths`: some request has 1023 cached tokens. `move_slot`: each row lists 4 distinct slots. `move_target`: each row lists 4 distinct row indices other than its own; every row index is named exactly 4 times, by distinct sources. `page_table`: the 13 x 8 entries of one device are each of 0 to 103 once.
All inputs are finite; a program needn't handle non-finite values.
Results may differ from a plain program's by a relative error of at most 0.011.
Values may be sent and summed in bfloat16 or wider, within the bound.
No kernel may reach another device: no remote copies, remote signals or barrier semaphores. Data moves between devices by JAX's collectives and lax.ppermute only.
A program may use at most 64 MiB of HBM per device.

v0:
```python
import functools

import jax
import jax.numpy as jnp
from jax import lax
from jax.experimental import pallas as pl
from jax.experimental.pallas import tpu as pltpu
from jax.sharding import PartitionSpec as P

HP = 64
NS = 256
KW = 4
QH = 8
KVH = 2
HD = 128
PAGE = 32
LANES = 128
BLOCK = 16

EPSILON = 1e-05
FLOOR_SCORE = -1e30
FIRST_LIMIT = 60 * 1024 * 1024
VMEM_LIMIT = 57 * 1024 * 1024
LAST_LIMIT = 24 * 1024 * 1024

F32 = jnp.float32
BF16 = jnp.bfloat16
I32 = jnp.int32

SMEM_SPEC = pl.BlockSpec(memory_space=pltpu.SMEM)
BRIEF = pl.CostEstimate(flops=1, bytes_accessed=1, transcendentals=0)
VMEM_SPEC = pl.BlockSpec(memory_space=pltpu.VMEM)
ANY_SPEC = pl.BlockSpec(memory_space=pl.ANY)


def silu(v):
    return v / (1.0 + jnp.exp(-v))


def dot(a, b):
    return jnp.dot(a, b, preferred_element_type=F32)


def dot_t(a, b):
    return lax.dot_general(a, b, (((1,), (1,)), ((), ())), preferred_element_type=F32)


def row_iota(shape):
    return lax.broadcasted_iota(I32, shape, 0)


def lane_iota(shape):
    return lax.broadcasted_iota(I32, shape, 1)


class Columns:
    def __init__(self, inner):
        self.z = 0
        self.x = inner
        self.bc = 2 * inner
        self.q = self.bc + 2 * NS
        self.kv = self.q + QH * HD
        self.tail = self.kv + 2 * KVH * HD
        self.width = self.tail + 2 * LANES


class Plan:
    def __init__(self, slots, moves):
        self.length = 0
        self.slot = slots
        self.target = self.slot + moves
        self.away = self.target + moves
        self.source = self.away + moves
        self.from_away = self.source + moves
        self.arrived_length = self.from_away + moves
        self.stay = self.arrived_length + moves
        self.me = self.stay + slots - moves
        self.size = self.me + 1


def early_parts(row_count):
    return [d for d in (2, 4) if d < row_count]


def parcel_parts(refs, row_count, pages_here):
    refs, early = list(refs), early_parts(row_count)
    parts = []
    for d in range(1, row_count):
        if d in early:
            parts.append((refs.pop(0), refs.pop(0)))
        else:
            whole = refs.pop(0)
            parts.append((whole.at[:pages_here], whole.at[pages_here:]))
    return parts


class Note:
    mixed, key_value, drive, drive_low, mixing, conv_x, conv_bc = 0, 1, 2, 3, 4, 5, 8
    decay, decay_low = NS, NS + LANES


def project_kernel(
    row_ref, arrival, lengths, move_slot, move_target, table,
    tokens, gain, w_z, w_x, w_dt, w_bc, w_qkv, pool, state,
    plan, mine, theirs, *rest,
):
    inverse, wide, picked, tail, packed, in_sems, out_sems = rest[-7:]
    moves, row_count = move_slot.shape
    pages_here, slots = table.shape
    parcels = parcel_parts(rest[:-7], row_count, pages_here)
    heads, depth = w_dt.shape
    inner = heads * HP
    cols, at = Columns(inner), Plan(slots, moves)
    me, half = row_ref[0], row_count // 2

    loads = []
    for m in range(moves):
        slot = move_slot[m, me]
        for page in range(pages_here):
            loads.append(
                pltpu.make_async_copy(pool.at[table[page, slot]], packed.at[m, page], in_sems.at[m, page])
            )
        for part in range(2):
            loads.append(
                pltpu.make_async_copy(
                    state.at[slot, :, part * PAGE : (part + 1) * PAGE, :],
                    packed.at[m, pages_here:, :, part * NS : (part + 1) * NS],
                    in_sems.at[m, pages_here + part],
                )
            )
    for load in loads:
        load.start()

    wide[...] = tokens[...].astype(F32)
    picked[...] = jnp.zeros_like(picked)

    def invert(t, carry):
        for s in range(slots):
            inverse[arrival[t * slots + s]] = t * slots + s
        return carry

    lax.fori_loop(0, row_count, invert, 0)

    def pick(b, carry):
        d = jnp.where(b < half, 2 * b, 2 * (b - half) + 1)
        first = lax.bitwise_xor(me, d) * slots
        for s in range(slots):
            picked[pl.ds(b * BLOCK + s, 1), :] = wide[pl.ds(inverse[first + s], 1), :]
        return carry

    lax.fori_loop(0, row_count, pick, 0)

    for load in loads:
        load.wait()

    def sent(m, to):
        pages, states = to
        return (
            pltpu.make_async_copy(packed.at[m, :pages_here], pages, out_sems.at[m, 0]),
            pltpu.make_async_copy(packed.at[m, pages_here:], states, out_sems.at[m, 1]),
        )

    for m in range(moves):
        away = lax.bitwise_xor(move_target[m, me], me)
        for d, parcel in enumerate(parcels, 1):

            @pl.when(away == d)
            def _(m=m, parcel=parcel):
                for copy in sent(m, parcel):
                    copy.start()

    rows = picked[...]
    squares = jnp.sum(rows * rows, axis=1, keepdims=True)
    scaled = (rows * gain[...].astype(F32).reshape(1, depth)).astype(BF16)

    def put(start, value):
        span = slice(start, start + value.shape[1])
        mine[:, span] = value[: half * BLOCK].astype(F32)
        theirs[:, span] = value[half * BLOCK :].astype(BF16)

    put(cols.z, dot(scaled, w_z[...]))
    put(cols.x, dot(scaled, w_x[...]))
    put(cols.bc, dot(scaled, w_bc[...]))
    put(cols.q, dot(scaled, w_qkv[...]))
    tail[...] = jnp.zeros_like(tail)
    tail[:, :heads] = dot_t(scaled, w_dt[...])
    tail[:, heads : heads + 1] = squares
    high = tail[...].astype(BF16)
    put(cols.tail, high)
    put(cols.tail + LANES, tail[...] - high.astype(F32))

    stays = 0
    for s in range(slots):
        plan[at.length + s] = lengths[me * slots + s]
        leaves = move_slot[0, me] == s
        for m in range(1, moves):
            leaves = jnp.logical_or(leaves, move_slot[m, me] == s)

        @pl.when(jnp.logical_not(leaves))
        def _(s=s, stays=stays):
            plan[at.stay + stays] = s

        stays = stays + jnp.where(leaves, 0, 1)
    for m in range(moves):
        plan[at.slot + m] = move_slot[m, me]
        plan[at.target + m] = move_target[m, me]
        plan[at.away + m] = lax.bitwise_xor(move_target[m, me], me)

    def seek(i, turn):
        for m in range(moves):
            comes = move_target[m, i] == me

            @pl.when(comes)
            def _(m=m, turn=turn):
                plan[at.source + turn] = i
                plan[at.from_away + turn] = lax.bitwise_xor(i, me)
                plan[at.arrived_length + turn] = lengths[i * slots + move_slot[m, i]]

            turn = turn + jnp.where(comes, 1, 0)
        return turn

    lax.fori_loop(0, row_count, seek, I32(0))
    plan[at.me] = me
    for m in range(moves):
        for copy in sent(m, parcels[0]):
            copy.wait()


def pair_kernel(mine, theirs, own, *others):
    for j, out in enumerate((own,) + others):
        span = slice(j * BLOCK, (j + 1) * BLOCK)
        out[...] = (mine[span, :] + theirs[span, :].astype(F32)).astype(out.dtype)


def widen(per_head, inner):
    rows = per_head.shape[0]
    first = lane_iota((rows, 2 * HP)) < HP
    pieces = []
    for h in range(0, inner // HP, 2):
        pieces.append(jnp.where(first, per_head[:, h : h + 1], per_head[:, h + 1 : h + 2]))
    return pieces[0] if len(pieces) == 1 else jnp.concatenate(pieces, axis=1)


class Sums:
    def __init__(self, received, heads, width):
        self.received = received
        cols = Columns(heads * HP)
        tail = self.total(cols.tail, cols.tail + LANES) + self.total(cols.tail + LANES, cols.width)
        self.root = jnp.sqrt(tail[:, heads : heads + 1] / width + EPSILON)
        self.step_in = (tail[:, :heads] / self.root).astype(BF16).astype(F32)

    def total(self, start, stop):
        return sum(part[:, start:stop].astype(F32) for part in self.received)

    def projected(self, start, stop):
        return (self.total(start, stop) / self.root).astype(BF16).astype(F32)


def inserted(page, row, offset):
    return jnp.where(row_iota(page.shape) == offset, row, page.astype(F32)).astype(BF16)


def place_of(length, col_count):
    logical = lax.div(length, I32(PAGE))
    return lax.rem(logical, I32(col_count)), lax.div(logical, I32(col_count)), lax.rem(length, I32(PAGE))


def attend_kernel(
    col_ref, plan, table, pool, *rest, moves, heads, chip_count, col_count, width
):
    received, (pool_next, kv_new, send) = rest[:chip_count], rest[chip_count : chip_count + 3]
    pages, queries, scores, weighted, peaks, totals, in_sems, out_sems = rest[chip_count + 3 :]
    pages_here, slots = table.shape
    cols, at = Columns(heads * HP), Plan(slots, moves)
    col = col_ref[0]
    tokens_here = pages_here * PAGE
    kv_width = KVH * HD
    chunks = in_sems.shape[0]
    step = pool.shape[0] // chunks
    spans = [pl.ds(k * step, step) for k in range(chunks)]
    loads = [pltpu.make_async_copy(pool.at[span], pages.at[span], in_sems.at[k]) for k, span in enumerate(spans)]
    for load in loads:
        load.start()

    sums = Sums(received, heads, width)
    kv_new[...] = sums.projected(cols.kv, cols.tail)
    q_in = sums.projected(cols.q, cols.kv)
    for h in range(QH):
        queries[pl.ds(h, BLOCK, stride=QH), :] = q_in[:, h * HD : (h + 1) * HD]

    first_group = row_iota((QH, HD)) < QH // KVH
    lane = lane_iota((QH, tokens_here))
    position = (lax.shift_right_logical(lane, 5) * col_count + col) * PAGE + lax.bitwise_and(lane, PAGE - 1)
    for load in loads:
        load.wait()
    for s in range(slots):
        owner, local_page, offset = place_of(plan[at.length + s], col_count)
        page = table[local_page, s]
        pages[page] = inserted(pages[page], kv_new[s : s + 1, :], jnp.where(owner == col, offset, -1))
    stores = [
        pltpu.make_async_copy(pages.at[span], pool_next.at[span], out_sems.at[k]) for k, span in enumerate(spans)
    ]
    for store in stores:
        store.start()

    def cached(s, start):
        parts = [pages[table[page, s], :, start : start + kv_width] for page in range(pages_here)]
        return jnp.concatenate(parts, axis=0)

    for s in range(slots):
        query = queries[s * QH : (s + 1) * QH, :]
        query = jnp.concatenate(
            [jnp.where(first_group, query, 0.0), jnp.where(first_group, 0.0, query)], axis=1
        ).astype(BF16)
        score = dot_t(query, cached(s, 0)) * (HD ** -0.5)
        scores[s * QH : (s + 1) * QH, :] = jnp.where(position <= plan[at.length + s], score, FLOOR_SCORE)

    live_rows = slots * QH
    everything = scores[0:live_rows, :]
    peak = jnp.max(everything, axis=1, keepdims=True)
    weights = jnp.where(everything > 0.5 * FLOOR_SCORE, jnp.exp(everything - peak), 0.0)
    total = jnp.sum(weights, axis=1, keepdims=True)
    scores[0:live_rows, :] = weights
    for ref, value in ((weighted, None), (peaks, peak), (totals, total)):
        ref[live_rows:, :] = jnp.zeros((BLOCK * QH - live_rows, HD), F32)
        if value is not None:
            ref[0:live_rows, :] = jnp.broadcast_to(value, (live_rows, HD))
    for s in range(slots):
        weight = scores[s * QH : (s + 1) * QH, :]
        high = weight.astype(BF16).astype(F32)
        both = dot(jnp.concatenate([high, weight - high], axis=0).astype(BF16), cached(s, kv_width))
        joined = both[:QH] + both[QH:]
        weighted[s * QH : (s + 1) * QH, :] = jnp.where(first_group, joined[:, :HD], joined[:, HD:])

    share = QH * HD // col_count
    part = min(share, HD)
    lanes = lane_iota((BLOCK, LANES))
    for c in range(col_count):
        block = slice(c * BLOCK, (c + 1) * BLOCK)
        stats = jnp.zeros((BLOCK, LANES), F32)
        for j in range(share // part):
            head, begin = divmod(c * share + j * part, HD)
            rows = pl.ds(head, BLOCK, stride=QH)
            send[block, j * part : (j + 1) * part] = weighted[rows, :][:, begin : begin + part]
            stats = jnp.where(lanes == 2 * j, peaks[rows, :], stats)
            stats = jnp.where(lanes == 2 * j + 1, totals[rows, :], stats)
        send[block, share:] = stats
    for store in stores:
        store.wait()


def mix_kernel(
    plan, conv_x, conv_bc, cw_x, cw_bc, dt_bias, a_log, d_skip, state, *rest, moves, chip_count, width
):
    received = rest[:chip_count]
    conv_x_next, conv_bc_next, state_next, gated, driven_out, decay, b_out = rest[chip_count : chip_count + 7]
    readout, held, made, drive, b_twice, in_sems, out_sems = rest[chip_count + 7 :]
    slots, inner = conv_x.shape[1], conv_x.shape[2]
    heads = dt_bias.shape[0]
    cols, at = Columns(inner), Plan(slots, moves)
    loads = []
    for s in range(slots):
        loads.append(pltpu.make_async_copy(state.at[s], held.at[s], in_sems.at[s]))
        loads[-1].start()

    sums = Sums(received, heads, width)

    def convolved(past, taps, fresh, following):
        past_rows = [past[k].astype(F32) for k in range(KW - 1)]
        total = fresh[:slots] * taps[KW - 1 : KW, :].astype(F32)
        for k in range(KW - 1):
            total = total + past_rows[k] * taps[k : k + 1, :].astype(F32)
            following[k] = past_rows[k + 1] if k < KW - 2 else fresh[:slots]
        return jnp.concatenate([silu(total), jnp.zeros((BLOCK - slots, total.shape[1]), F32)], axis=0)

    value_act = convolved(conv_x, cw_x, sums.projected(cols.x, cols.bc), conv_x_next)
    bc_act = convolved(conv_bc, cw_bc, sums.projected(cols.bc, cols.q), conv_bc_next)
    bc_act = bc_act.astype(BF16).astype(F32)
    b_in, c_val = bc_act[:, :NS], bc_act[:, NS:]
    b_out[...] = b_in
    b_twice[...] = jnp.concatenate([b_in, b_in], axis=0)
    c_out = c_val.astype(BF16)

    shifted = sums.step_in + dt_bias[...].reshape(1, heads)
    step_size = jnp.maximum(shifted, 0.0) + jnp.log(1.0 + jnp.exp(-jnp.abs(shifted)))
    rate = jnp.exp(-jnp.exp(a_log[...].reshape(1, heads)) * step_size)
    decay[...] = rate
    driven = widen(step_size, inner) * value_act
    driven_out[...] = driven
    high = driven.astype(BF16).astype(F32)
    drive[...] = jnp.transpose(jnp.concatenate([high, driven - high], axis=0)).astype(BF16)

    readout[...] = jnp.zeros_like(readout)

    for s in range(slots):
        loads[s].wait()
        value = dot_t(c_out, held[s].reshape(inner, NS))
        readout[s : s + 1, :] = value[s : s + 1]

    stores = []
    for j in range(slots - moves):
        slot = plan[at.stay + j]
        advance_state(slot, held.at[slot], b_twice, drive, decay, made.at[j])
        stores.append(pltpu.make_async_copy(made.at[j], state_next.at[slot], out_sems.at[j]))
        stores[-1].start()

    gate = silu(sums.projected(cols.z, cols.x))
    b_dot_c = jnp.sum(b_in * c_val, axis=1, keepdims=True)
    skip = widen(jnp.broadcast_to(d_skip[...].reshape(1, heads), (BLOCK, heads)), inner)
    total = widen(rate, inner) * readout[...] + driven * b_dot_c + skip * value_act
    gated[...] = (total * gate).astype(BF16).astype(F32)
    for store in stores:
        store.wait()


def advance_state(slot, prior, b_twice, drive, decay, result):
    heads = result.shape[0]
    twice = b_twice[...]
    half = twice.shape[0] // 2
    row = row_iota(twice.shape)
    selected = jnp.where((row == slot) | (row == slot + half), twice, 0.0).astype(BF16)
    outer = dot(drive[...], selected).reshape(heads, HP, NS)
    for h in range(heads):
        rate = decay[pl.ds(slot, 1), h : h + 1]
        result[h] = (rate * prior[h].astype(F32) + outer[h]).astype(BF16)


def output_kernel(
    gated, w_ssm_all, w_attn_all, partials, send, w_ssm, w_attn, sems, *, slots, col_count
):
    columns = w_ssm.shape[1] // col_count
    spans = [slice(c * columns, (c + 1) * columns) for c in range(col_count)]
    loads = [
        [
            pltpu.make_async_copy(whole.at[:, span], held.at[:, span], sems.at[c, k])
            for k, (whole, held) in enumerate(((w_ssm_all, w_ssm), (w_attn_all, w_attn)))
        ]
        for c, span in enumerate(spans)
    ]
    for load in loads:
        load[0].start()
        load[1].start()
    share = w_attn.shape[0]
    part = min(share, HD)
    blocks = [partials[c * BLOCK : (c + 1) * BLOCK, :] for c in range(col_count)]
    pieces = []
    for j in range(share // part):
        peaks = [b[:, share + 2 * j : share + 2 * j + 1] for b in blocks]
        joint = functools.reduce(jnp.maximum, peaks)
        factors = [jnp.exp(p - joint) for p in peaks]
        total = sum(f * b[:, share + 2 * j + 1 : share + 2 * j + 2] for f, b in zip(factors, blocks))
        value = sum(f * b[:, j * part : (j + 1) * part] for f, b in zip(factors, blocks))
        pieces.append(value / total)
    joined = pieces[0] if len(pieces) == 1 else jnp.concatenate(pieces, axis=1)
    right = jnp.where(row_iota(joined.shape) < slots, joined, 0.0).astype(BF16)
    left = gated[...].astype(BF16)
    for c, span in enumerate(spans):
        loads[c][0].wait()
        loads[c][1].wait()
        terms = dot(left, w_ssm[:, span]) + dot(right, w_attn[:, span])
        send[c * BLOCK : (c + 1) * BLOCK, :] = terms.astype(BF16)


def total_kernel(
    plan, kv_new, driven, decay, b_in, conv_x, conv_bc, terms, send, mixed, block, *, moves, col_count
):
    at = Plan(conv_x.shape[1], moves)
    total = sum(terms[c * BLOCK : (c + 1) * BLOCK, :].astype(F32) for c in range(col_count))
    mixed[...] = total
    send[pl.ds(pl.multiple_of(plan[at.me] * BLOCK, BLOCK), BLOCK), : total.shape[1]] = total.astype(BF16)

    block[...] = jnp.zeros_like(block)
    for m in range(moves):
        row = pl.ds(plan[at.slot + m], 1)

        def put(index, value, start=0):
            block[index : index + 1, start : start + value.shape[1]] = value

        put(Note.mixed, mixed[row, :])
        put(Note.key_value, kv_new[row, :])
        for index, value, start, low_index, low_start in (
            (Note.drive, driven[row, :], 0, Note.drive_low, 0),
            (Note.mixing, decay[row, :], Note.decay, Note.mixing, Note.decay_low),
        ):
            high = value.astype(BF16).astype(F32)
            put(index, high, start)
            put(low_index, value - high, low_start)
        put(Note.mixing, b_in[row, :])
        for k in range(KW - 1):
            put(Note.conv_x + k, conv_x[k, row, :])
            put(Note.conv_bc + k, conv_bc[k, row, :])
        start = pl.multiple_of(plan[at.target + m] * BLOCK, BLOCK)
        send[pl.ds(start, BLOCK), :] = block[...].astype(BF16)


def arrive_kernel(
    col_ref, plan, table, conv_x, conv_bc, state_in, pool_in, notes, *rest,
    moves, row_count, col_count,
):
    del state_in, pool_in
    parcel_count = row_count - 1 + len(early_parts(row_count))
    parcels, rest = rest[:parcel_count], rest[parcel_count:]
    pages_here, slots = table.shape
    inner = conv_x.shape[2]
    heads = inner // HP
    at = Plan(slots, moves)
    mixed, conv_x_next, conv_bc_next, state_next, pool_next = rest[:5]
    packed, made, drive, decay, b_twice, window_x, window_bc, window_mixed, in_sems, out_sems = rest[5:]
    col = col_ref[0]
    parcels = parcel_parts(parcels, row_count, pages_here)

    def loaded(m, parcel):
        pages, states = parcel
        return (
            pltpu.make_async_copy(pages, packed.at[m, :pages_here], in_sems.at[m, 0]),
            pltpu.make_async_copy(states, packed.at[m, pages_here:], in_sems.at[m, 1]),
        )

    for m in range(moves):
        for d, parcel in enumerate(parcels, 1):

            @pl.when(plan[at.from_away + m] == d)
            def _(m=m, parcel=parcel):
                for copy in loaded(m, parcel):
                    copy.start()


    for k in range(KW - 1):
        window_x[k] = conv_x[k]
        window_bc[k] = conv_bc[k]
    home = pl.multiple_of(plan[at.me] * BLOCK, BLOCK)
    window_mixed[...] = notes[pl.ds(home, BLOCK), : window_mixed.shape[1]].astype(F32)
    rows = []
    b_twice[...] = jnp.zeros_like(b_twice)
    half = b_twice.shape[0] // 2
    for m in range(moves):
        start = pl.multiple_of(plan[at.source + m] * BLOCK, BLOCK)
        note = notes[pl.ds(start, BLOCK), :].astype(F32)
        rows.append(note)
        row = pl.ds(plan[at.slot + m], 1)
        window_mixed[row, :] = note[Note.mixed : Note.mixed + 1, : window_mixed.shape[1]]
        for k in range(KW - 1):
            window_x[k, row, :] = note[Note.conv_x + k : Note.conv_x + k + 1, :inner]
            window_bc[k, row, :] = note[Note.conv_bc + k : Note.conv_bc + k + 1, : 2 * NS]
        mixing = note[Note.mixing : Note.mixing + 1, :]
        b_twice[m : m + 1, :] = mixing[:, :NS]
        b_twice[half + m : half + m + 1, :] = mixing[:, :NS]
        decay[m : m + 1, :] = (
            mixing[:, Note.decay : Note.decay + heads] + mixing[:, Note.decay_low : Note.decay_low + heads]
        )
    padding = [jnp.zeros((half - moves, inner), F32)]
    stacked = [note[Note.drive : Note.drive + 1, :inner] for note in rows] + padding
    stacked += [note[Note.drive_low : Note.drive_low + 1, :inner] for note in rows] + padding
    drive[...] = jnp.transpose(jnp.concatenate(stacked, axis=0)).astype(BF16)
    mixed[...] = window_mixed[0:slots, :].astype(BF16)
    for k in range(KW - 1):
        conv_x_next[k] = window_x[k].astype(BF16)
        conv_bc_next[k] = window_bc[k].astype(BF16)

    stores = []
    for m in range(moves):
        slot = plan[at.slot + m]
        for copy in loaded(m, parcels[0]):
            copy.wait()
        owner, local_page, offset = place_of(plan[at.arrived_length + m], col_count)
        key_value = rows[m][Note.key_value : Note.key_value + 1, : 2 * KVH * HD]

        @pl.when(owner == col)
        def _(m=m, local_page=local_page, offset=offset, key_value=key_value):
            packed[m, local_page] = inserted(packed[m, local_page], key_value, offset)

        for page in range(pages_here):
            stores.append(
                pltpu.make_async_copy(
                    packed.at[m, page], pool_next.at[table[page, slot]], out_sems.at[m, page]
                )
            )
            stores[-1].start()
        prior = [
            jnp.concatenate([packed[m, pages_here + h, :, :NS], packed[m, pages_here + h, :, NS:]], axis=0)
            for h in range(heads)
        ]
        advance_state(m, prior, b_twice, drive, decay, made.at[m])
        stores.append(pltpu.make_async_copy(made.at[m], state_next.at[slot], out_sems.at[m, pages_here]))
        stores[-1].start()
    for store in stores:
        store.wait()


def shape(dims, dtype):
    return jax.ShapeDtypeStruct(tuple(dims), dtype)


def params(limit=VMEM_LIMIT):
    return pltpu.CompilerParams(vmem_limit_bytes=limit)


def exchange(value, axis):
    return lax.all_to_all(value, axis, split_axis=0, concat_axis=0, tiled=True)


def trade(block, axis, d):
    return lax.ppermute(block, axis, [(i, i ^ d) for i in range(lax.axis_size(axis))])


def ordered(value, first):
    return lax.optimization_barrier((value, first))[0]


def local(
    tokens, arrival, cache_lengths, move_slot, move_target, page_table, kv_pool, ssm_state,
    conv_x, conv_bc, norm_gain, weight_z, weight_x, weight_dt, weight_bc, weight_qkv,
    conv_weight_x, conv_weight_bc, dt_bias, a_log, d_skip, weight_ssm_out, weight_attn_out,
):
    row_count = lax.axis_size("rows")
    col_count = lax.axis_size("cols")
    row_index = lax.axis_index("rows").astype(I32).reshape(1)
    col_index = lax.axis_index("cols").astype(I32).reshape(1)
    slots, heads = ssm_state.shape[0], ssm_state.shape[1]
    total, depth = tokens.shape
    moves = move_slot.shape[1]
    pages_here, width = page_table.shape[3], kv_pool.shape[3]
    inner = heads * HP
    stays = slots - moves
    cols, at = Columns(inner), Plan(slots, moves)
    table = page_table[0, 0].T
    pool = kv_pool[:, 0]
    past_x, past_bc = conv_x.transpose(1, 0, 2), conv_bc.transpose(1, 0, 2)
    rows = row_count * BLOCK
    model = depth * row_count
    share = QH * HD // col_count
    parcel = (pages_here + heads, PAGE, width)
    parcels_here = pltpu.VMEM((moves,) + parcel, BF16)

    chip_count = row_count // 2
    early = early_parts(row_count)
    parcels_out = []
    for d in range(1, row_count):
        if d in early:
            parcels_out += [shape((pages_here,) + parcel[1:], BF16), shape((heads,) + parcel[1:], BF16)]
        else:
            parcels_out.append(shape(parcel, BF16))
    plan, mine, theirs, *parcels = pl.pallas_call(
        project_kernel,
        out_shape=[
            shape((at.size,), I32),
            shape((chip_count * BLOCK, cols.width), F32),
            shape((chip_count * BLOCK, cols.width), BF16),
        ]
        + parcels_out,
        in_specs=[SMEM_SPEC] * 6 + [VMEM_SPEC] * 7 + [ANY_SPEC] * 2,
        out_specs=[SMEM_SPEC] + [VMEM_SPEC] * 2 + [ANY_SPEC] * len(parcels_out),
        scratch_shapes=[
            pltpu.SMEM((total,), I32),
            pltpu.VMEM((total, depth), F32),
            pltpu.VMEM((rows, depth), F32),
            pltpu.VMEM((rows, LANES), F32),
            parcels_here,
            pltpu.SemaphoreType.DMA((moves, pages_here + 2)),
            pltpu.SemaphoreType.DMA((moves, 2)),
        ],
        compiler_params=params(FIRST_LIMIT),
        cost_estimate=BRIEF,
        name="project",
    )(
        row_index, arrival, cache_lengths, move_slot.T, move_target.T, table,
        tokens, norm_gain, weight_z, weight_x, weight_dt.T, weight_bc, weight_qkv, pool, ssm_state,
    )
    moving = {}
    for d in range(1, row_count):
        moving[d] = [parcels.pop(0) for _ in range(2 if d in early else 1)]
    ahead = []
    for d in early:
        moving[d][0] = trade(moving[d][0], "rows", d)
        ahead.append(moving[d][0])

    sums = pl.pallas_call(
        pair_kernel,
        out_shape=[shape((BLOCK, cols.width), F32)] + [shape((BLOCK, cols.width), BF16)] * (chip_count - 1),
        in_specs=[VMEM_SPEC] * 2,
        out_specs=[VMEM_SPEC] * chip_count,
        compiler_params=params(FIRST_LIMIT),
        cost_estimate=BRIEF,
        name="pair",
    )(mine, trade(theirs, "rows", 1))
    received = [sums[0]] + [trade(block, "rows", 2 * j) for j, block in enumerate(sums[1:], 1)]

    def migrate(parts, after):
        for d in parts:
            moving[d][-1] = trade(ordered(moving[d][-1], after), "rows", d)

    order = [d for j in range(2) for d in range(2 + j, row_count, 2)] + [1]
    received = ordered(received, ahead)
    migrate(order[:-2], received)

    pool_next, kv_new, partials = pl.pallas_call(
        functools.partial(
            attend_kernel, moves=moves, heads=heads, chip_count=chip_count, col_count=col_count, width=model
        ),
        out_shape=[
            shape(pool.shape, BF16),
            shape((BLOCK, 2 * KVH * HD), F32),
            shape((col_count * BLOCK, share + LANES), F32),
        ],
        in_specs=[SMEM_SPEC] * 3 + [ANY_SPEC] + [VMEM_SPEC] * chip_count,
        out_specs=[ANY_SPEC] + [VMEM_SPEC] * 2,
        scratch_shapes=[
            pltpu.VMEM(pool.shape, BF16),
            pltpu.VMEM((BLOCK * QH, HD), F32),
            pltpu.VMEM((BLOCK * QH, pages_here * PAGE), F32),
            pltpu.VMEM((BLOCK * QH, HD), F32),
            pltpu.VMEM((BLOCK * QH, HD), F32),
            pltpu.VMEM((BLOCK * QH, HD), F32),
            pltpu.SemaphoreType.DMA((2 if pool.shape[0] % 4 else 4,)),
            pltpu.SemaphoreType.DMA((2 if pool.shape[0] % 4 else 4,)),
        ],
        compiler_params=params(),
        cost_estimate=BRIEF,
        name="attend",
    )(col_index, plan, table, pool, *received)
    received = ordered(received, partials)
    partials = exchange(partials, "cols")

    next_x, next_bc, state_next, gated, driven, decay, b_in = pl.pallas_call(
        functools.partial(mix_kernel, moves=moves, chip_count=chip_count, width=model),
        out_shape=(
            shape(past_x.shape, F32),
            shape(past_bc.shape, F32),
            shape(ssm_state.shape, BF16),
            shape((BLOCK, inner), F32),
            shape((BLOCK, inner), F32),
            shape((BLOCK, heads), F32),
            shape((BLOCK, NS), F32),
        ),
        in_specs=[SMEM_SPEC] + [VMEM_SPEC] * 7 + [ANY_SPEC] + [VMEM_SPEC] * chip_count,
        out_specs=(VMEM_SPEC, VMEM_SPEC, ANY_SPEC) + (VMEM_SPEC,) * 4,
        scratch_shapes=[
            pltpu.VMEM((BLOCK, inner), F32),
            pltpu.VMEM((slots, heads, HP, NS), BF16),
            pltpu.VMEM((stays, heads, HP, NS), BF16),
            pltpu.VMEM((inner, 2 * BLOCK), BF16),
            pltpu.VMEM((2 * BLOCK, NS), F32),
            pltpu.SemaphoreType.DMA((slots,)),
            pltpu.SemaphoreType.DMA((stays,)),
        ],
        compiler_params=params(),
        cost_estimate=BRIEF,
        name="mix",
    )(plan, past_x, past_bc, conv_weight_x, conv_weight_bc, dt_bias, a_log, d_skip, ssm_state, *received)

    columns = weight_ssm_out.shape[1] // col_count
    terms = pl.pallas_call(
        functools.partial(output_kernel, slots=slots, col_count=col_count),
        out_shape=shape((col_count * BLOCK, columns), BF16),
        in_specs=[VMEM_SPEC] + [ANY_SPEC] * 2 + [VMEM_SPEC],
        out_specs=VMEM_SPEC,
        scratch_shapes=[
            pltpu.VMEM(weight_ssm_out.shape, BF16),
            pltpu.VMEM(weight_attn_out.shape, BF16),
            pltpu.SemaphoreType.DMA((col_count, 2)),
        ],
        compiler_params=params(FIRST_LIMIT),
        cost_estimate=BRIEF,
        name="output",
    )(gated, weight_ssm_out, weight_attn_out, partials)
    migrate(order[-2:], terms)
    terms = exchange(terms, "cols")

    note = (BLOCK, max(inner, 2 * NS, 2 * KVH * HD, columns))
    notes = pl.pallas_call(
        functools.partial(total_kernel, moves=moves, col_count=col_count),
        out_shape=shape((rows, note[1]), BF16),
        in_specs=[SMEM_SPEC] + [VMEM_SPEC] * 7,
        out_specs=VMEM_SPEC,
        scratch_shapes=[pltpu.VMEM((BLOCK, columns), F32), pltpu.VMEM(note, F32)],
        compiler_params=params(),
        cost_estimate=BRIEF,
        name="total",
    )(plan, kv_new, driven, decay, b_in, next_x, next_bc, terms)
    notes = exchange(notes, "rows")

    mixed, conv_x_next, conv_bc_next, state_next, pool_next = pl.pallas_call(
        functools.partial(arrive_kernel, moves=moves, row_count=row_count, col_count=col_count),
        out_shape=(
            shape((slots, columns), BF16),
            shape(past_x.shape, BF16),
            shape(past_bc.shape, BF16),
            shape(ssm_state.shape, BF16),
            shape(pool.shape, BF16),
        ),
        in_specs=[SMEM_SPEC] * 3 + [VMEM_SPEC] * 2 + [ANY_SPEC] * 2 + [VMEM_SPEC] + [ANY_SPEC] * len(parcels_out),
        out_specs=[VMEM_SPEC] * 3 + [ANY_SPEC] * 2,
        scratch_shapes=[
            parcels_here,
            pltpu.VMEM((moves, heads, HP, NS), BF16),
            pltpu.VMEM((inner, 2 * BLOCK), BF16),
            pltpu.VMEM((BLOCK, heads), F32),
            pltpu.VMEM((2 * BLOCK, NS), F32),
            pltpu.VMEM((KW - 1, slots, inner), F32),
            pltpu.VMEM((KW - 1, slots, 2 * NS), F32),
            pltpu.VMEM((BLOCK, columns), F32),
            pltpu.SemaphoreType.DMA((moves, 2)),
            pltpu.SemaphoreType.DMA((moves, pages_here + 1)),
        ],
        input_output_aliases={5: 3, 6: 4},
        compiler_params=params(LAST_LIMIT),
        cost_estimate=BRIEF,
        name="arrive",
    )(
        col_index, plan, table, next_x, next_bc, state_next, pool_next, notes,
        *(part for d in range(1, row_count) for part in moving[d]),
    )
    return (
        mixed, state_next, conv_x_next.transpose(1, 0, 2), conv_bc_next.transpose(1, 0, 2), pool_next[:, None]
    )


def solution(mesh):
    in_specs = (
        P(None, "rows"),
        P(),
        P(),
        P(),
        P(),
        P("rows", "cols", None, None),
        P("rows", "cols", None, None),
        P("rows", "cols", None, None),
        P("rows", None, "cols"),
        P("rows", None, None),
        P("rows"),
        P("rows", "cols"),
        P("rows", "cols"),
        P("rows", "cols"),
        P("rows", None),
        P("rows", None),
        P(None, "cols"),
        P(),
        P("cols"),
        P("cols"),
        P("cols"),
        P("cols", None),
        P("cols", None),
    )
    out_specs = (
        P("rows", "cols"),
        P("rows", "cols", None, None),
        P("rows", None, "cols"),
        P("rows", None, None),
        P("rows", "cols", None, None),
    )
    return jax.shard_map(local, mesh=mesh, in_specs=in_specs, out_specs=out_specs, check_vma=False)
```

profile of v0, /device:TPU:0, one launch (start us, length us, event | category | flops | bytes accessed | tf_op | source)
XLA Modules:
  0.0 78.3 jit_solution(12021967212902008958)
XLA Ops:
  0.6 6.0 %project.1 = (s32[47]{0:T(128)}, f32[64,3328]{1,0:T(8,128)}, bf16[64,3328]{1,0:T(8,128)(2,1)}, bf16[16,32,512]{2,1,0:T(8,128)(2,1)}, bf16[8,32,512]{2,1,0:T(8,12...) custom-call(s32[1]{0:T(128)} %bitcast.1.row_ref, ...), custom_call_target="tpu_custom_call" | custom-call | flops 1 | bytes 1 | tf_op jit(solution)/shard_map/project/pallas_call | solution.py:643
  7.2 2.6 %collective-permute-start.4 = (bf16[8,32,512]{2,1,0:T(8,128)(2,1)}, bf16[8,32,512]{2,1,0:T(8,128)(2,1)S(1)}, u32[]{:S(2)}, u32[]{:S(2)}) collective-permute-start(bf16[8,32,512]{2,1,0:T(8,128)(2,1)} %get-tuple-element.58), channel_id=1, source_target_pairs={{0,8},{4,12},{8,0},{12,4},{16,24},{20,28},{24,16},{28,20},{1,9},{5... | collective-permute-start | bytes 786440 | tf_op jit(solution)/shard_map/ppermute | solution.py:603
  9.8 1.5 %collective-permute-start.5 = (bf16[8,32,512]{2,1,0:T(8,128)(2,1)}, bf16[8,32,512]{2,1,0:T(8,128)(2,1)S(1)}, u32[]{:S(2)}, u32[]{:S(2)}) collective-permute-start(bf16[8,32,512]{2,1,0:T(8,128)(2,1)} %get-tuple-element.59), channel_id=1, source_target_pairs={{0,16},{4,20},{8,24},{12,28},{16,0},{20,4},{24,8},{28,12},{1,17},{... | collective-permute-start | bytes 786440 | tf_op jit(solution)/shard_map/ppermute | solution.py:603
  11.3 0.8 copy-done.4
  12.0 2.1 %pair.1 = (f32[16,3328]{1,0:T(8,128)}, bf16[16,3328]{1,0:T(8,128)(2,1)}, bf16[16,3328]{1,0:T(8,128)(2,1)}, bf16[16,3328]{1,0:T(8,128)(2,1)}) custom-call(f32[64,3328]{1,0:T(8,128)} %get-tuple-element.52.mine, bf16[64,3328]{1,0:T(8,128)(2,1)} %copy-done.4), custom_call_target="tpu_custom_call" | custom-call | flops 1 | bytes 1 | tf_op jit(solution)/shard_map/pair/pallas_call | solution.py:677
  14.6 1.4 %collective-permute-start.2 = (bf16[16,3328]{1,0:T(8,128)(2,1)}, bf16[16,3328]{1,0:T(8,128)(2,1)S(1)}, u32[]{:S(2)}, u32[]{:S(2)}) collective-permute-start(bf16[16,3328]{1,0:T(8,128)(2,1)} %get-tuple-element.56), channel_id=1, source_target_pairs={{0,16},{4,20},{8,24},{12,28},{16,0},{20,4},{24,8},{28,12},{1,17},{... | collective-permute-start | bytes 319496 | tf_op jit(solution)/shard_map/ppermute | solution.py:603
  16.0 1.6 %collective-permute-start.3 = (bf16[16,3328]{1,0:T(8,128)(2,1)}, bf16[16,3328]{1,0:T(8,128)(2,1)S(1)}, u32[]{:S(2)}, u32[]{:S(2)}) collective-permute-start(bf16[16,3328]{1,0:T(8,128)(2,1)} %get-tuple-element.57), channel_id=1, source_target_pairs={{0,24},{4,28},{8,16},{12,20},{16,8},{20,12},{24,0},{28,4},{1,25},{... | collective-permute-start | bytes 319496 | tf_op jit(solution)/shard_map/ppermute | solution.py:603
  17.6 1.5 %collective-permute-done.5.rest_4_ = bf16[8,32,512]{2,1,0:T(8,128)(2,1)S(1)} collective-permute-done((bf16[8,32,512]{2,1,0:T(8,128)(2,1)}, bf16[8,32,512]{2,1,0:T(8,128)(2,1)S(1)}, u32[]{:S(2)}, u32[]{:S(2)}) %collective-permute-start.5) | collective-permute-done | bytes 262176 | tf_op jit(solution)/shard_map/ppermute | solution.py:603
  19.1 0.9 %collective-permute-done.1.rest_1_ = bf16[16,3328]{1,0:T(8,128)(2,1)S(1)} collective-permute-done((bf16[16,3328]{1,0:T(8,128)(2,1)}, bf16[16,3328]{1,0:T(8,128)(2,1)S(1)}, u32[]{:S(2)}, u32[]{:S(2)}) %collective-permute-start.1) | collective-permute-done | bytes 106528 | tf_op jit(solution)/shard_map/ppermute | solution.py:603
  20.0 2.9 %collective-permute-done.2.rest_2_ = bf16[16,3328]{1,0:T(8,128)(2,1)S(1)} collective-permute-done((bf16[16,3328]{1,0:T(8,128)(2,1)}, bf16[16,3328]{1,0:T(8,128)(2,1)S(1)}, u32[]{:S(2)}, u32[]{:S(2)}) %collective-permute-start.2) | collective-permute-done | bytes 106528 | tf_op jit(solution)/shard_map/ppermute | solution.py:603
  22.9 1.2 %collective-permute-start.7 = (bf16[8,32,512]{2,1,0:T(8,128)(2,1)}, bf16[8,32,512]{2,1,0:T(8,128)(2,1)S(1)}, u32[]{:S(2)}, u32[]{:S(2)}) collective-permute-start(bf16[8,32,512]{2,1,0:T(8,128)(2,1)} %get-tuple-element.81), channel_id=1, source_target_pairs={{0,8},{4,12},{8,0},{12,4},{16,24},{20,28},{24,16},{28,20},{1,9},{5... | collective-permute-start | bytes 786440 | tf_op jit(solution)/shard_map/ppermute | solution.py:603
  24.1 0.9 %collective-permute-start.9 = (bf16[8,32,512]{2,1,0:T(8,128)(2,1)}, bf16[8,32,512]{2,1,0:T(8,128)(2,1)S(1)}, u32[]{:S(2)}, u32[]{:S(2)}) collective-permute-start(bf16[8,32,512]{2,1,0:T(8,128)(2,1)} %get-tuple-element.85), channel_id=1, source_target_pairs={{0,16},{4,20},{8,24},{12,28},{16,0},{20,4},{24,8},{28,12},{1,17},{... | collective-permute-start | bytes 786440 | tf_op jit(solution)/shard_map/ppermute | solution.py:603
  25.0 6.0 %attend.1 = (bf16[104,32,512]{2,1,0:T(8,128)(2,1)}, f32[16,512]{1,0:T(8,128)}, f32[64,384]{1,0:T(8,128)}) custom-call(s32[1]{0:T(128)} %bitcast.col_ref, s32[47]{0:T(128)} %get-tuple-element.51.plan, s32[8,13]{1,0:T(8,128)} %bitcast.24, bf16[104,32,512]{2,1,0:T(8,128)(2,1)} %bitcast.27, f32[16,3328]{1,0:T(8,128)} %get-tuple-element.65.rest_0_, ...), custom_call_target="tpu_custom_call" | custom-call | flops 1 | bytes 1 | tf_op jit(solution)/shard_map/attend/pallas_call | solution.py:696
  31.0 4.9 %all-to-all-start = ((f32[4,16,384]{2,1,0:T(8,128)}), f32[4,16,384]{2,1,0:T(8,128)S(1)}, u32[]{:S(2)}, u32[]{:S(2)}) async-start(f32[4,16,384]{2,1,0:T(8,128)} %bitcast.33), calls=%async_computation | async-start | bytes 196608 | tf_op jit(solution)/shard_map/all_to_all | solution.py:599
  35.9 1.8 %collective-permute-start.10 = (bf16[16,32,512]{2,1,0:T(8,128)(2,1)}, bf16[16,32,512]{2,1,0:T(8,128)(2,1)S(1)}, u32[]{:S(2)}, u32[]{:S(2)}) collective-permute-start(bf16[16,32,512]{2,1,0:T(8,128)(2,1)} %get-tuple-element.87), channel_id=1, source_target_pairs={{0,20},{4,16},{8,28},{12,24},{16,4},{20,0},{24,12},{28,8},{1,21},{... | collective-permute-start | bytes 1572872 | tf_op jit(solution)/shard_map/ppermute | solution.py:603
  37.6 1.5 %collective-permute-start.11 = (bf16[16,32,512]{2,1,0:T(8,128)(2,1)}, bf16[16,32,512]{2,1,0:T(8,128)(2,1)S(1)}, u32[]{:S(2)}, u32[]{:S(2)}) collective-permute-start(bf16[16,32,512]{2,1,0:T(8,128)(2,1)} %get-tuple-element.89), channel_id=1, source_target_pairs={{0,24},{4,28},{8,16},{12,20},{16,8},{20,12},{24,0},{28,4},{1,25},{... | collective-permute-start | bytes 1572872 | tf_op jit(solution)/shard_map/ppermute | solution.py:603
  39.1 7.2 %mix.1 = (f32[3,13,512]{2,1,0:T(8,128)}, f32[3,13,512]{2,1,0:T(8,128)}, bf16[13,8,64,256]{3,2,1,0:T(8,128)(2,1)}, f32[16,512]{1,0:T(8,128)}, f32[16,512]{1,0:T(8...) custom-call(s32[47]{0:T(128)} %get-tuple-element.51.plan, bf16[3,13,512]{2,1,0:T(8,128)(2,1)} %bitcast.34, ...), custom_call_target="tpu_custom_call" | custom-call | flops 1 | bytes 1 | tf_op jit(solution)/shard_map/mix/pallas_call | solution.py:724
  46.3 0.6 copy-done.8
  47.0 3.7 %output.1 = bf16[64,512]{1,0:T(8,128)(2,1)} custom-call(f32[16,512]{1,0:T(8,128)} %get-tuple-element.77.gated, bf16[512,2048]{1,0:T(8,128)(2,1)} %w_ssm_all.1, bf16[256,2048]{1,0:T(8,128)(2,1)} %w_attn_all.1, f32[64,384]{1,0:T(8,128)} %bitcast.30), custom_call_target="tpu_custom_call" | custom-call | flops 1 | bytes 1 | tf_op jit(solution)/shard_map/output/pallas_call | solution.py:752
  50.8 1.6 %collective-permute-start.12 = (bf16[16,32,512]{2,1,0:T(8,128)(2,1)S(1)}, bf16[16,32,512]{2,1,0:T(8,128)(2,1)S(1)}, u32[]{:S(2)}, u32[]{:S(2)}) collective-permute-start(bf16[16,32,512]{2,1,0:T(8,128)(2,1)S(1)} %copy-done.9), channel_id=1, source_target_pairs={{0,28},{4,24},{8,20},{12,16},{16,12},{20,8},{24,4},{28,0},{1,29},{... | collective-permute-start | bytes 1572872 | tf_op jit(solution)/shard_map/ppermute | solution.py:603
  52.4 10.9 %all_to_all.33 = bf16[4,16,512]{2,1,0:T(8,128)(2,1)} all-to-all(bf16[4,16,512]{2,1,0:T(8,128)(2,1)} %bitcast.31), channel_id=1, replica_groups=mesh['rows'=8,'cols'=4] {'cols'}, dimensions={0} | all-to-all | bytes 131072 | tf_op jit(solution)/shard_map/all_to_all | solution.py:599
  63.3 1.7 %total.1 = bf16[128,512]{1,0:T(8,128)(2,1)} custom-call(s32[47]{0:T(128)} %get-tuple-element.51.plan, f32[16,512]{1,0:T(8,128)} %get-tuple-element.73.kv_new, f32[16,512]{1,0:T(8,128)} %get-tuple-element.74.driven, f32[16,8]{1,0:T(8,128)} %get-tuple-element.75.decay, f32[16,256]{1,0:T(8,128)} %get-tuple-element.76.b_in, ...), custom_call_target="tpu_custom_call" | custom-call | flops 1 | bytes 1 | tf_op jit(solution)/shard_map/total/pallas_call | solution.py:770
  65.0 9.2 %all_to_all.34 = bf16[8,16,512]{2,1,0:T(8,128)(2,1)S(1)} all-to-all(bf16[8,16,512]{2,1,0:T(8,128)(2,1)} %bitcast.29), channel_id=1, replica_groups=mesh['rows'=8,'cols'=4] {'rows'}, dimensions={0} | all-to-all | bytes 262144 | tf_op jit(solution)/shard_map/all_to_all | solution.py:599
  74.3 4.0 %arrive.1 = (bf16[13,512]{1,0:T(8,128)(2,1)}, bf16[3,13,512]{2,1,0:T(8,128)(2,1)}, bf16[3,13,512]{2,1,0:T(8,128)(2,1)}, bf16[13,8,64,256]{3,2,1,0:T(8,128)(2,1)}, bf16[104,32,512]{2,1,0:T(8,128)(2,1)}) custom-call(s32[1]{0:T(128)} %bitcast.col_ref, s32[47]{0:T(128)S(1)} %copy-done.3, ...), custom_call_target="tpu_custom_call", output_to_operand_aliasing={{3}: (5, {}), {4}: (6, {})} | custom-call | flops 1 | bytes 1 | tf_op jit(solution)/shard_map/arrive/pallas_call | solution.py:782
  (33 shorter events, 1.2 us)
Async XLA Ops:
  6.6 4.6 %collective-permute-start = (bf16[64,3328]{1,0:T(8,128)(2,1)}, bf16[64,3328]{1,0:T(8,128)(2,1)S(1)}, u32[]{:S(2)}, u32[]{:S(2)}) collective-permute-start(bf16[64,3328]{1,0:T(8,128)(2,1)} %get-tuple-element.53), channel_id=1, source_target_pairs={{0,4},{4,0},{8,12},{12,8},{16,20},{20,16},{24,28},{28,24},{1,5},{5... | collective-permute-start | bytes 1277960 | tf_op jit(solution)/shard_map/ppermute | solution.py:603
  7.2 10.4 %collective-permute-start.4 = (bf16[8,32,512]{2,1,0:T(8,128)(2,1)}, bf16[8,32,512]{2,1,0:T(8,128)(2,1)S(1)}, u32[]{:S(2)}, u32[]{:S(2)}) collective-permute-start(bf16[8,32,512]{2,1,0:T(8,128)(2,1)} %get-tuple-element.58), channel_id=1, source_target_pairs={{0,8},{4,12},{8,0},{12,4},{16,24},{20,28},{24,16},{28,20},{1,9},{5... | collective-permute-start | bytes 786440 | tf_op jit(solution)/shard_map/ppermute | solution.py:603
  9.8 9.4 %collective-permute-start.5 = (bf16[8,32,512]{2,1,0:T(8,128)(2,1)}, bf16[8,32,512]{2,1,0:T(8,128)(2,1)S(1)}, u32[]{:S(2)}, u32[]{:S(2)}) collective-permute-start(bf16[8,32,512]{2,1,0:T(8,128)(2,1)} %get-tuple-element.59), channel_id=1, source_target_pairs={{0,16},{4,20},{8,24},{12,28},{16,0},{20,4},{24,8},{28,12},{1,17},{... | collective-permute-start | bytes 786440 | tf_op jit(solution)/shard_map/ppermute | solution.py:603
  11.3 0.8 copy-start.4
  14.1 5.9 %collective-permute-start.1 = (bf16[16,3328]{1,0:T(8,128)(2,1)}, bf16[16,3328]{1,0:T(8,128)(2,1)S(1)}, u32[]{:S(2)}, u32[]{:S(2)}) collective-permute-start(bf16[16,3328]{1,0:T(8,128)(2,1)} %get-tuple-element.55), channel_id=1, source_target_pairs={{0,8},{4,12},{8,0},{12,4},{16,24},{20,28},{24,16},{28,20},{1,9},{5... | collective-permute-start | bytes 319496 | tf_op jit(solution)/shard_map/ppermute | solution.py:603
  14.6 8.3 %collective-permute-start.2 = (bf16[16,3328]{1,0:T(8,128)(2,1)}, bf16[16,3328]{1,0:T(8,128)(2,1)S(1)}, u32[]{:S(2)}, u32[]{:S(2)}) collective-permute-start(bf16[16,3328]{1,0:T(8,128)(2,1)} %get-tuple-element.56), channel_id=1, source_target_pairs={{0,16},{4,20},{8,24},{12,28},{16,0},{20,4},{24,8},{28,12},{1,17},{... | collective-permute-start | bytes 319496 | tf_op jit(solution)/shard_map/ppermute | solution.py:603
  16.0 6.9 %collective-permute-start.3 = (bf16[16,3328]{1,0:T(8,128)(2,1)}, bf16[16,3328]{1,0:T(8,128)(2,1)S(1)}, u32[]{:S(2)}, u32[]{:S(2)}) collective-permute-start(bf16[16,3328]{1,0:T(8,128)(2,1)} %get-tuple-element.57), channel_id=1, source_target_pairs={{0,24},{4,28},{8,16},{12,20},{16,8},{20,12},{24,0},{28,4},{1,25},{... | collective-permute-start | bytes 319496 | tf_op jit(solution)/shard_map/ppermute | solution.py:603
  20.0 5.0 %copy-start.5 = (bf16[16,3328]{1,0:T(8,128)(2,1)}, bf16[16,3328]{1,0:T(8,128)(2,1)S(1)}, u32[]{:S(2)}) copy-start(bf16[16,3328]{1,0:T(8,128)(2,1)S(1)} %collective-permute-done.1.rest_1_) | copy-start | bytes 319492
  22.9 2.1 %copy-start.6 = (bf16[16,3328]{1,0:T(8,128)(2,1)}, bf16[16,3328]{1,0:T(8,128)(2,1)S(1)}, u32[]{:S(2)}) copy-start(bf16[16,3328]{1,0:T(8,128)(2,1)S(1)} %collective-permute-done.2.rest_2_) | copy-start | bytes 319492
  22.9 2.1 %copy-start.7 = (bf16[16,3328]{1,0:T(8,128)(2,1)}, bf16[16,3328]{1,0:T(8,128)(2,1)S(1)}, u32[]{:S(2)}) copy-start(bf16[16,3328]{1,0:T(8,128)(2,1)S(1)} %collective-permute-done.3.rest_3_) | copy-start | bytes 319492
  22.9 27.8 %collective-permute-start.7 = (bf16[8,32,512]{2,1,0:T(8,128)(2,1)}, bf16[8,32,512]{2,1,0:T(8,128)(2,1)S(1)}, u32[]{:S(2)}, u32[]{:S(2)}) collective-permute-start(bf16[8,32,512]{2,1,0:T(8,128)(2,1)} %get-tuple-element.81), channel_id=1, source_target_pairs={{0,8},{4,12},{8,0},{12,4},{16,24},{20,28},{24,16},{28,20},{1,9},{5... | collective-permute-start | bytes 786440 | tf_op jit(solution)/shard_map/ppermute | solution.py:603
  24.1 26.7 %collective-permute-start.9 = (bf16[8,32,512]{2,1,0:T(8,128)(2,1)}, bf16[8,32,512]{2,1,0:T(8,128)(2,1)S(1)}, u32[]{:S(2)}, u32[]{:S(2)}) collective-permute-start(bf16[8,32,512]{2,1,0:T(8,128)(2,1)} %get-tuple-element.85), channel_id=1, source_target_pairs={{0,16},{4,20},{8,24},{12,28},{16,0},{20,4},{24,8},{28,12},{1,17},{... | collective-permute-start | bytes 786440 | tf_op jit(solution)/shard_map/ppermute | solution.py:603
  31.0 15.3 %all-to-all-start = ((f32[4,16,384]{2,1,0:T(8,128)}), f32[4,16,384]{2,1,0:T(8,128)S(1)}, u32[]{:S(2)}, u32[]{:S(2)}) async-start(f32[4,16,384]{2,1,0:T(8,128)} %bitcast.33), calls=%async_computation | async-start | bytes 196608 | tf_op jit(solution)/shard_map/all_to_all | solution.py:599
  35.9 38.3 %collective-permute-start.8 = (bf16[16,32,512]{2,1,0:T(8,128)(2,1)}, bf16[16,32,512]{2,1,0:T(8,128)(2,1)S(1)}, u32[]{:S(2)}, u32[]{:S(2)}) collective-permute-start(bf16[16,32,512]{2,1,0:T(8,128)(2,1)} %get-tuple-element.83), channel_id=1, source_target_pairs={{0,12},{4,8},{8,4},{12,0},{16,28},{20,24},{24,20},{28,16},{1,13},{... | collective-permute-start | bytes 1572872 | tf_op jit(solution)/shard_map/ppermute | solution.py:603
  35.9 38.3 %collective-permute-start.10 = (bf16[16,32,512]{2,1,0:T(8,128)(2,1)}, bf16[16,32,512]{2,1,0:T(8,128)(2,1)S(1)}, u32[]{:S(2)}, u32[]{:S(2)}) collective-permute-start(bf16[16,32,512]{2,1,0:T(8,128)(2,1)} %get-tuple-element.87), channel_id=1, source_target_pairs={{0,20},{4,16},{8,28},{12,24},{16,4},{20,0},{24,12},{28,8},{1,21},{... | collective-permute-start | bytes 1572872 | tf_op jit(solution)/shard_map/ppermute | solution.py:603
  37.6 36.6 %collective-permute-start.11 = (bf16[16,32,512]{2,1,0:T(8,128)(2,1)}, bf16[16,32,512]{2,1,0:T(8,128)(2,1)S(1)}, u32[]{:S(2)}, u32[]{:S(2)}) collective-permute-start(bf16[16,32,512]{2,1,0:T(8,128)(2,1)} %get-tuple-element.89), channel_id=1, source_target_pairs={{0,24},{4,28},{8,16},{12,20},{16,8},{20,12},{24,0},{28,4},{1,25},{... | collective-permute-start | bytes 1572872 | tf_op jit(solution)/shard_map/ppermute | solution.py:603
  39.1 11.7 %copy-start.9 = (bf16[16,32,512]{2,1,0:T(8,128)(2,1)S(1)}, bf16[16,32,512]{2,1,0:T(8,128)(2,1)}, u32[]{:S(2)}) copy-start(bf16[16,32,512]{2,1,0:T(8,128)(2,1)} %get-tuple-element.91) | copy-start | bytes 1572868
  39.1 35.2 %copy-start.2 = (s32[1,1,13,8]{2,3,1,0:T(8,128)S(1)}, s32[1,1,13,8]{2,3,1,0:T(8,128)}, u32[]{:S(2)}) copy-start(s32[1,1,13,8]{2,3,1,0:T(8,128)} %param.28) | copy-start | bytes 1252
  39.1 35.2 %copy-start.3 = (s32[47]{0:T(128)S(1)}, s32[47]{0:T(128)}, u32[]{:S(2)}) copy-start(s32[47]{0:T(128)} %get-tuple-element.51.plan) | copy-start | bytes 568
  46.3 28.0 %copy-start = (f32[3,13,512]{2,1,0:T(8,128)S(1)}, f32[3,13,512]{2,1,0:T(8,128)}, u32[]{:S(2)}) copy-start(f32[3,13,512]{2,1,0:T(8,128)} %get-tuple-element.69.conv_x) | copy-start | bytes 239620
  46.3 28.0 %copy-start.1 = (f32[3,13,512]{2,1,0:T(8,128)S(1)}, f32[3,13,512]{2,1,0:T(8,128)}, u32[]{:S(2)}) copy-start(f32[3,13,512]{2,1,0:T(8,128)} %get-tuple-element.70.conv_bc) | copy-start | bytes 239620
  46.3 0.7 copy-start.8
  50.7 23.5 %collective-permute-start.6 = (bf16[16,32,512]{2,1,0:T(8,128)(2,1)}, bf16[16,32,512]{2,1,0:T(8,128)(2,1)S(1)}, u32[]{:S(2)}, u32[]{:S(2)}) collective-permute-start(bf16[16,32,512]{2,1,0:T(8,128)(2,1)} %get-tuple-element.79), channel_id=1, source_target_pairs={{0,4},{4,0},{8,12},{12,8},{16,20},{20,16},{24,28},{28,24},{1,5},{5... | collective-permute-start | bytes 1572872 | tf_op jit(solution)/shard_map/ppermute | solution.py:603
  50.8 23.4 %collective-permute-start.12 = (bf16[16,32,512]{2,1,0:T(8,128)(2,1)S(1)}, bf16[16,32,512]{2,1,0:T(8,128)(2,1)S(1)}, u32[]{:S(2)}, u32[]{:S(2)}) collective-permute-start(bf16[16,32,512]{2,1,0:T(8,128)(2,1)S(1)} %copy-done.9), channel_id=1, source_target_pairs={{0,28},{4,24},{8,20},{12,16},{16,12},{20,8},{24,4},{28,0},{1,29},{... | collective-permute-start | bytes 1572872 | tf_op jit(solution)/shard_map/ppermute | solution.py:603
where the time goes:
time: 78.9 us; the launch traced here: 78.3 us
  Pallas kernels  30.6 us (39%)
  blocking collectives  20.1 us (25%)
  starting transfers between devices  19.9 us (25%)
  waiting for transfers between devices  5.36 us (7%)
  local copies, waits for them, and re-layouts  1.43 us (2%)
  between operations  0.81 us (1%)
    all_to_all x2, blocking collectives, exchange(): return lax.all_to_all(value, axis, split_axis=0, concat_axis=0, tiled=True)  20.1 us
    ppermute x13, starting transfers between devices, trade(): lax.ppermute(block, axis, [(i, i ^ d) for i in range(lax.axis_size(axis))])  15.1 us
    pallas_call x1, Pallas kernels, local(): pl.pallas_call(functools.partial(mix_kernel, moves=moves, chip_count=chip...  7.19 us
    pallas_call x1, Pallas kernels, local(): pl.pallas_call(functools.partial(attend_kernel, moves=moves, heads=heads,...  5.99 us
    pallas_call x1, Pallas kernels, local(): pl.pallas_call(project_kernel, out_shape=[shape((at.size,), I32), shape((...  5.97 us
    ppermute x13, waiting for transfers between devices, trade(): lax.ppermute(block, axis, [(i, i ^ d) for i in range(lax.axis_size(axis))])  5.35 us
    all_to_all x1, starting transfers between devices, exchange(): return lax.all_to_all(value, axis, split_axis=0, concat_axis=0, tiled=True)  4.88 us
    pallas_call x1, Pallas kernels, local(): pl.pallas_call(functools.partial(arrive_kernel, moves=moves, row_count=ro...  3.97 us
  transfers between devices with their start and end apart: 14, of which 3 were waited for; matrix products, arithmetic and copies ran while one was open for 0% of the time, Pallas kernels for 26%

commit v1 on v0

--- a/solution.py
+++ b/solution.py
@@ -118,14 +118,14 @@
         slot = move_slot[m, me]
         for page in range(pages_here):
             loads.append(
-                pltpu.make_async_copy(pool.at[table[page, slot]], packed.at[m, page], in_sems.at[m, page])
+                pltpu.make_async_copy(pool.at[table[page, slot]], packed.at[m, page], in_sems.at[m])
             )
         for part in range(2):
             loads.append(
                 pltpu.make_async_copy(
                     state.at[slot, :, part * PAGE : (part + 1) * PAGE, :],
                     packed.at[m, pages_here:, :, part * NS : (part + 1) * NS],
-                    in_sems.at[m, pages_here + part],
+                    in_sems.at[m],
                 )
             )
     for load in loads:
@@ -150,8 +150,8 @@
 
     lax.fori_loop(0, row_count, pick, 0)
 
-    for load in loads:
-        load.wait()
+    for m in range(moves):
+        pltpu.make_async_copy(pool.at[: pages_here + heads], packed.at[m], in_sems.at[m]).wait()
 
     def sent(m, to):
         pages, states = to
@@ -350,14 +350,14 @@
 
 
 def mix_kernel(
-    plan, conv_x, conv_bc, cw_x, cw_bc, dt_bias, a_log, d_skip, state, *rest, moves, chip_count, width
+    conv_x, conv_bc, cw_x, cw_bc, dt_bias, a_log, d_skip, state, *rest, chip_count, width
 ):
     received = rest[:chip_count]
-    conv_x_next, conv_bc_next, state_next, gated, driven_out, decay, b_out = rest[chip_count : chip_count + 7]
-    readout, held, made, drive, b_twice, in_sems, out_sems = rest[chip_count + 7 :]
+    conv_x_next, conv_bc_next, gated, driven_out, decay, drive, b_twice = rest[chip_count : chip_count + 7]
+    readout, held, in_sems = rest[chip_count + 7 :]
     slots, inner = conv_x.shape[1], conv_x.shape[2]
     heads = dt_bias.shape[0]
-    cols, at = Columns(inner), Plan(slots, moves)
+    cols = Columns(inner)
     loads = []
     for s in range(slots):
         loads.append(pltpu.make_async_copy(state.at[s], held.at[s], in_sems.at[s]))
@@ -377,7 +377,6 @@
     bc_act = convolved(conv_bc, cw_bc, sums.projected(cols.bc, cols.q), conv_bc_next)
     bc_act = bc_act.astype(BF16).astype(F32)
     b_in, c_val = bc_act[:, :NS], bc_act[:, NS:]
-    b_out[...] = b_in
     b_twice[...] = jnp.concatenate([b_in, b_in], axis=0)
     c_out = c_val.astype(BF16)
 
@@ -397,18 +396,27 @@
         value = dot_t(c_out, held[s].reshape(inner, NS))
         readout[s : s + 1, :] = value[s : s + 1]
 
-    stores = []
-    for j in range(slots - moves):
-        slot = plan[at.stay + j]
-        advance_state(slot, held.at[slot], b_twice, drive, decay, made.at[j])
-        stores.append(pltpu.make_async_copy(made.at[j], state_next.at[slot], out_sems.at[j]))
-        stores[-1].start()
-
     gate = silu(sums.projected(cols.z, cols.x))
     b_dot_c = jnp.sum(b_in * c_val, axis=1, keepdims=True)
     skip = widen(jnp.broadcast_to(d_skip[...].reshape(1, heads), (BLOCK, heads)), inner)
     total = widen(rate, inner) * readout[...] + driven * b_dot_c + skip * value_act
     gated[...] = (total * gate).astype(BF16).astype(F32)
+
+
+def stay_kernel(plan, drive, decay, b_twice, state, state_next, held, made, in_sems, out_sems, *, moves):
+    stays = held.shape[0]
+    at = Plan(state.shape[0], moves)
+    loads = []
+    for j in range(stays):
+        loads.append(pltpu.make_async_copy(state.at[plan[at.stay + j]], held.at[j], in_sems.at[j]))
+        loads[-1].start()
+    stores = []
+    for j in range(stays):
+        slot = plan[at.stay + j]
+        loads[j].wait()
+        advance_state(slot, held.at[j], b_twice, drive, decay, made.at[j])
+        stores.append(pltpu.make_async_copy(made.at[j], state_next.at[slot], out_sems.at[j]))
+        stores[-1].start()
     for store in stores:
         store.wait()
 
@@ -425,21 +433,7 @@
         result[h] = (rate * prior[h].astype(F32) + outer[h]).astype(BF16)
 
 
-def output_kernel(
-    gated, w_ssm_all, w_attn_all, partials, send, w_ssm, w_attn, sems, *, slots, col_count
-):
-    columns = w_ssm.shape[1] // col_count
-    spans = [slice(c * columns, (c + 1) * columns) for c in range(col_count)]
-    loads = [
-        [
-            pltpu.make_async_copy(whole.at[:, span], held.at[:, span], sems.at[c, k])
-            for k, (whole, held) in enumerate(((w_ssm_all, w_ssm), (w_attn_all, w_attn)))
-        ]
-        for c, span in enumerate(spans)
-    ]
-    for load in loads:
-        load[0].start()
-        load[1].start()
+def output_kernel(gated, w_ssm, w_attn, partials, send, *, slots, col_count):
     share = w_attn.shape[0]
     part = min(share, HD)
     blocks = [partials[c * BLOCK : (c + 1) * BLOCK, :] for c in range(col_count)]
@@ -454,15 +448,15 @@
     joined = pieces[0] if len(pieces) == 1 else jnp.concatenate(pieces, axis=1)
     right = jnp.where(row_iota(joined.shape) < slots, joined, 0.0).astype(BF16)
     left = gated[...].astype(BF16)
-    for c, span in enumerate(spans):
-        loads[c][0].wait()
-        loads[c][1].wait()
+    columns = w_ssm.shape[1] // col_count
+    for c in range(col_count):
+        span = slice(c * columns, (c + 1) * columns)
         terms = dot(left, w_ssm[:, span]) + dot(right, w_attn[:, span])
         send[c * BLOCK : (c + 1) * BLOCK, :] = terms.astype(BF16)
 
 
 def total_kernel(
-    plan, kv_new, driven, decay, b_in, conv_x, conv_bc, terms, send, mixed, block, *, moves, col_count
+    plan, kv_new, driven, decay, b_twice, conv_x, conv_bc, terms, send, mixed, block, *, moves, col_count
 ):
     at = Plan(conv_x.shape[1], moves)
     total = sum(terms[c * BLOCK : (c + 1) * BLOCK, :].astype(F32) for c in range(col_count))
@@ -485,7 +479,7 @@
             high = value.astype(BF16).astype(F32)
             put(index, high, start)
             put(low_index, value - high, low_start)
-        put(Note.mixing, b_in[row, :])
+        put(Note.mixing, b_twice[row, :])
         for k in range(KW - 1):
             put(Note.conv_x + k, conv_x[k, row, :])
             put(Note.conv_bc + k, conv_bc[k, row, :])
@@ -656,7 +650,7 @@
             pltpu.VMEM((rows, depth), F32),
             pltpu.VMEM((rows, LANES), F32),
             parcels_here,
-            pltpu.SemaphoreType.DMA((moves, pages_here + 2)),
+            pltpu.SemaphoreType.DMA((moves,)),
             pltpu.SemaphoreType.DMA((moves, 2)),
         ],
         compiler_params=params(FIRST_LIMIT),
@@ -721,50 +715,57 @@
     received = ordered(received, partials)
     partials = exchange(partials, "cols")
 
-    next_x, next_bc, state_next, gated, driven, decay, b_in = pl.pallas_call(
-        functools.partial(mix_kernel, moves=moves, chip_count=chip_count, width=model),
+    next_x, next_bc, gated, driven, decay, drive, b_twice = pl.pallas_call(
+        functools.partial(mix_kernel, chip_count=chip_count, width=model),
         out_shape=(
             shape(past_x.shape, F32),
             shape(past_bc.shape, F32),
-            shape(ssm_state.shape, BF16),
             shape((BLOCK, inner), F32),
             shape((BLOCK, inner), F32),
             shape((BLOCK, heads), F32),
-            shape((BLOCK, NS), F32),
+            shape((inner, 2 * BLOCK), BF16),
+            shape((2 * BLOCK, NS), F32),
         ),
-        in_specs=[SMEM_SPEC] + [VMEM_SPEC] * 7 + [ANY_SPEC] + [VMEM_SPEC] * chip_count,
-        out_specs=(VMEM_SPEC, VMEM_SPEC, ANY_SPEC) + (VMEM_SPEC,) * 4,
+        in_specs=[VMEM_SPEC] * 7 + [ANY_SPEC] + [VMEM_SPEC] * chip_count,
+        out_specs=(VMEM_SPEC,) * 7,
         scratch_shapes=[
             pltpu.VMEM((BLOCK, inner), F32),
             pltpu.VMEM((slots, heads, HP, NS), BF16),
+            pltpu.SemaphoreType.DMA((slots,)),
+        ],
+        compiler_params=params(),
+        cost_estimate=BRIEF,
+        name="mix",
+    )(past_x, past_bc, conv_weight_x, conv_weight_bc, dt_bias, a_log, d_skip, ssm_state, *received)
+
+    columns = weight_ssm_out.shape[1] // col_count
+    terms = pl.pallas_call(
+        functools.partial(output_kernel, slots=slots, col_count=col_count),
+        out_shape=shape((col_count * BLOCK, columns), BF16),
+        in_specs=[VMEM_SPEC] * 4,
+        out_specs=VMEM_SPEC,
+        compiler_params=params(),
+        cost_estimate=BRIEF,
+        name="output",
+    )(gated, weight_ssm_out, weight_attn_out, partials)
+    migrate(order[-2:], terms)
+    drive = ordered(drive, terms)
+    terms = exchange(terms, "cols")
+    state_next = pl.pallas_call(
+        functools.partial(stay_kernel, moves=moves),
+        out_shape=shape(ssm_state.shape, BF16),
+        in_specs=[SMEM_SPEC] + [VMEM_SPEC] * 3 + [ANY_SPEC],
+        out_specs=ANY_SPEC,
+        scratch_shapes=[
             pltpu.VMEM((stays, heads, HP, NS), BF16),
-            pltpu.VMEM((inner, 2 * BLOCK), BF16),
-            pltpu.VMEM((2 * BLOCK, NS), F32),
-            pltpu.SemaphoreType.DMA((slots,)),
+            pltpu.VMEM((stays, heads, HP, NS), BF16),
+            pltpu.SemaphoreType.DMA((stays,)),
             pltpu.SemaphoreType.DMA((stays,)),
         ],
         compiler_params=params(),
         cost_estimate=BRIEF,
-        name="mix",
-    )(plan, past_x, past_bc, conv_weight_x, conv_weight_bc, dt_bias, a_log, d_skip, ssm_state, *received)
-
-    columns = weight_ssm_out.shape[1] // col_count
-    terms = pl.pallas_call(
-        functools.partial(output_kernel, slots=slots, col_count=col_count),
-        out_shape=shape((col_count * BLOCK, columns), BF16),
-        in_specs=[VMEM_SPEC] + [ANY_SPEC] * 2 + [VMEM_SPEC],
-        out_specs=VMEM_SPEC,
-        scratch_shapes=[
-            pltpu.VMEM(weight_ssm_out.shape, BF16),
-            pltpu.VMEM(weight_attn_out.shape, BF16),
-            pltpu.SemaphoreType.DMA((col_count, 2)),
-        ],
-        compiler_params=params(FIRST_LIMIT),
-        cost_estimate=BRIEF,
-        name="output",
-    )(gated, weight_ssm_out, weight_attn_out, partials)
-    migrate(order[-2:], terms)
-    terms = exchange(terms, "cols")
+        name="stay",
+    )(plan, drive, decay, b_twice, ssm_state)
 
     note = (BLOCK, max(inner, 2 * NS, 2 * KVH * HD, columns))
     notes = pl.pallas_call(
@@ -776,7 +777,7 @@
         compiler_params=params(),
         cost_estimate=BRIEF,
         name="total",
-    )(plan, kv_new, driven, decay, b_in, next_x, next_bc, terms)
+    )(plan, kv_new, driven, decay, b_twice, next_x, next_bc, terms)
     notes = exchange(notes, "rows")
 
     mixed, conv_x_next, conv_bc_next, state_next, pool_next = pl.pallas_call(

time: 78.9 us -> 80.5 us (1.020)
  blocking collectives: 20.1 us -> 10.9 us
  local copies, waits for them, and re-layouts: 1.43 us -> 4.73 us
  starting transfers between devices: 19.9 us -> 23.2 us
  Pallas kernels: 30.6 us -> 33.2 us
  waiting for transfers between devices: 5.36 us -> 6.94 us
    all_to_all x2 -> x1, blocking collectives: 20.1 us -> 10.9 us  [exchange(): return lax.all_to_all(value, axis, split_axis=0, concat_axis=0, tiled=True)]
    pallas_call x1 -> x2, Pallas kernels: 7.19 us -> 10.6 us  [the longest x1 5.39 us: local(): pl.pallas_call(functools.partial(mix_kernel, chip_count=chip_count, width...]
    all_to_all x1 -> x2, starting transfers between devices: 4.88 us -> 8.25 us  [exchange(): return lax.all_to_all(value, axis, split_axis=0, concat_axis=0, tiled=True)]
    unnamed x20 -> x26, local copies, waits for them, and re-layouts: 1.43 us -> 4.73 us
    all_to_all x1 -> x2, waiting for transfers between devices: 0.01 us -> 1.62 us  [exchange(): return lax.all_to_all(value, axis, split_axis=0, concat_axis=0, tiled=True)]
  transfers between devices with their start and end apart: 14 -> 15, of which waited for: 3 -> 4; matrix products, arithmetic and copies ran while one was open for 0% -> 0% of each run, Pallas kernels for 26% -> 30%
where the time goes in v1:
time: 80.5 us; the launch traced here: 79.8 us
  Pallas kernels  33.2 us (41%)
  starting transfers between devices  23.2 us (29%)
  blocking collectives  10.9 us (14%)
  waiting for transfers between devices  6.94 us (9%)
  local copies, waits for them, and re-layouts  4.73 us (6%)
  between operations  0.81 us (1%)
    ppermute x13, starting transfers between devices, trade(): lax.ppermute(block, axis, [(i, i ^ d) for i in range(lax.axis_size(axis))])  15 us
    all_to_all x1, blocking collectives, exchange(): return lax.all_to_all(value, axis, split_axis=0, concat_axis=0, tiled=True)  10.9 us
    all_to_all x2, starting transfers between devices, exchange(): return lax.all_to_all(value, axis, split_axis=0, concat_axis=0, tiled=True)  8.25 us
    pallas_call x1, Pallas kernels, local(): pl.pallas_call(functools.partial(attend_kernel, moves=moves, heads=heads,...  5.99 us
    pallas_call x1, Pallas kernels, local(): pl.pallas_call(project_kernel, out_shape=[shape((at.size,), I32), shape((...  5.68 us
    pallas_call x1, Pallas kernels, local(): pl.pallas_call(functools.partial(mix_kernel, chip_count=chip_count, width...  5.39 us
    ppermute x13, waiting for transfers between devices, trade(): lax.ppermute(block, axis, [(i, i ^ d) for i in range(lax.axis_size(axis))])  5.32 us
    pallas_call x1, Pallas kernels, local(): pl.pallas_call(functools.partial(stay_kernel, moves=moves), out_shape=sha...  5.23 us
  transfers between devices with their start and end apart: 15, of which 4 were waited for; matrix products, arithmetic and copies ran while one was open for 0% of the time, Pallas kernels for 30%

profile of v1, /device:TPU:0, one launch (start us, length us, event | category | flops | bytes accessed | tf_op | source)
XLA Modules:
  0.0 79.8 jit_solution(12759003448363423464)
XLA Ops:
  0.6 5.7 %project.1 = (s32[47]{0:T(128)}, f32[64,3328]{1,0:T(8,128)}, bf16[64,3328]{1,0:T(8,128)(2,1)}, bf16[16,32,512]{2,1,0:T(8,128)(2,1)}, bf16[8,32,512]{2,1,0:T(8,12...) custom-call(s32[1]{0:T(128)} %bitcast.1.row_ref, ...), custom_call_target="tpu_custom_call" | custom-call | flops 1 | bytes 1 | tf_op jit(solution)/shard_map/project/pallas_call | solution.py:637
  6.8 2.6 %collective-permute-start.4 = (bf16[8,32,512]{2,1,0:T(8,128)(2,1)}, bf16[8,32,512]{2,1,0:T(8,128)(2,1)S(1)}, u32[]{:S(2)}, u32[]{:S(2)}) collective-permute-start(bf16[8,32,512]{2,1,0:T(8,128)(2,1)} %get-tuple-element.59), channel_id=1, source_target_pairs={{0,8},{4,12},{8,0},{12,4},{16,24},{20,28},{24,16},{28,20},{1,9},{5... | collective-permute-start | bytes 786440 | tf_op jit(solution)/shard_map/ppermute | solution.py:597
  9.4 1.5 %collective-permute-start.5 = (bf16[8,32,512]{2,1,0:T(8,128)(2,1)}, bf16[8,32,512]{2,1,0:T(8,128)(2,1)S(1)}, u32[]{:S(2)}, u32[]{:S(2)}) collective-permute-start(bf16[8,32,512]{2,1,0:T(8,128)(2,1)} %get-tuple-element.60), channel_id=1, source_target_pairs={{0,16},{4,20},{8,24},{12,28},{16,0},{20,4},{24,8},{28,12},{1,17},{... | collective-permute-start | bytes 786440 | tf_op jit(solution)/shard_map/ppermute | solution.py:597
  11.7 2.1 %pair.1 = (f32[16,3328]{1,0:T(8,128)}, bf16[16,3328]{1,0:T(8,128)(2,1)}, bf16[16,3328]{1,0:T(8,128)(2,1)}, bf16[16,3328]{1,0:T(8,128)(2,1)}) custom-call(f32[64,3328]{1,0:T(8,128)} %get-tuple-element.53.mine, bf16[64,3328]{1,0:T(8,128)(2,1)} %copy-done.8), custom_call_target="tpu_custom_call" | custom-call | flops 1 | bytes 1 | tf_op jit(solution)/shard_map/pair/pallas_call | solution.py:671
  14.3 1.4 %collective-permute-start.2 = (bf16[16,3328]{1,0:T(8,128)(2,1)}, bf16[16,3328]{1,0:T(8,128)(2,1)S(1)}, u32[]{:S(2)}, u32[]{:S(2)}) collective-permute-start(bf16[16,3328]{1,0:T(8,128)(2,1)} %get-tuple-element.57), channel_id=1, source_target_pairs={{0,16},{4,20},{8,24},{12,28},{16,0},{20,4},{24,8},{28,12},{1,17},{... | collective-permute-start | bytes 319496 | tf_op jit(solution)/shard_map/ppermute | solution.py:597
  15.7 1.6 %collective-permute-start.3 = (bf16[16,3328]{1,0:T(8,128)(2,1)}, bf16[16,3328]{1,0:T(8,128)(2,1)S(1)}, u32[]{:S(2)}, u32[]{:S(2)}) collective-permute-start(bf16[16,3328]{1,0:T(8,128)(2,1)} %get-tuple-element.58), channel_id=1, source_target_pairs={{0,24},{4,28},{8,16},{12,20},{16,8},{20,12},{24,0},{28,4},{1,25},{... | collective-permute-start | bytes 319496 | tf_op jit(solution)/shard_map/ppermute | solution.py:597
  17.3 1.5 %collective-permute-done.5.rest_4_ = bf16[8,32,512]{2,1,0:T(8,128)(2,1)S(1)} collective-permute-done((bf16[8,32,512]{2,1,0:T(8,128)(2,1)}, bf16[8,32,512]{2,1,0:T(8,128)(2,1)S(1)}, u32[]{:S(2)}, u32[]{:S(2)}) %collective-permute-start.5) | collective-permute-done | bytes 262176 | tf_op jit(solution)/shard_map/ppermute | solution.py:597
  19.7 2.9 %collective-permute-done.2.rest_2_ = bf16[16,3328]{1,0:T(8,128)(2,1)S(1)} collective-permute-done((bf16[16,3328]{1,0:T(8,128)(2,1)}, bf16[16,3328]{1,0:T(8,128)(2,1)S(1)}, u32[]{:S(2)}, u32[]{:S(2)}) %collective-permute-start.2) | collective-permute-done | bytes 106528 | tf_op jit(solution)/shard_map/ppermute | solution.py:597
  22.6 1.2 %collective-permute-start.7 = (bf16[8,32,512]{2,1,0:T(8,128)(2,1)}, bf16[8,32,512]{2,1,0:T(8,128)(2,1)S(1)}, u32[]{:S(2)}, u32[]{:S(2)}) collective-permute-start(bf16[8,32,512]{2,1,0:T(8,128)(2,1)} %get-tuple-element.83), channel_id=1, source_target_pairs={{0,8},{4,12},{8,0},{12,4},{16,24},{20,28},{24,16},{28,20},{1,9},{5... | collective-permute-start | bytes 786440 | tf_op jit(solution)/shard_map/ppermute | solution.py:597
  24.7 6.0 %attend.1 = (bf16[104,32,512]{2,1,0:T(8,128)(2,1)}, f32[16,512]{1,0:T(8,128)}, f32[64,384]{1,0:T(8,128)}) custom-call(s32[1]{0:T(128)} %bitcast.col_ref, s32[47]{0:T(128)} %get-tuple-element.52.plan, s32[8,13]{1,0:T(8,128)} %bitcast.24, bf16[104,32,512]{2,1,0:T(8,128)(2,1)} %bitcast.27, f32[16,3328]{1,0:T(8,128)} %get-tuple-element.66.rest_0_, ...), custom_call_target="tpu_custom_call" | custom-call | flops 1 | bytes 1 | tf_op jit(solution)/shard_map/attend/pallas_call | solution.py:690
  30.7 4.9 %all-to-all-start = ((f32[4,16,384]{2,1,0:T(8,128)}), f32[4,16,384]{2,1,0:T(8,128)S(1)}, u32[]{:S(2)}, u32[]{:S(2)}) async-start(f32[4,16,384]{2,1,0:T(8,128)} %bitcast.33), calls=%async_computation | async-start | bytes 196608 | tf_op jit(solution)/shard_map/all_to_all | solution.py:593
  35.6 1.7 %collective-permute-start.10 = (bf16[16,32,512]{2,1,0:T(8,128)(2,1)}, bf16[16,32,512]{2,1,0:T(8,128)(2,1)S(1)}, u32[]{:S(2)}, u32[]{:S(2)}) collective-permute-start(bf16[16,32,512]{2,1,0:T(8,128)(2,1)} %get-tuple-element.89), channel_id=1, source_target_pairs={{0,20},{4,16},{8,28},{12,24},{16,4},{20,0},{24,12},{28,8},{1,21},{... | collective-permute-start | bytes 1572872 | tf_op jit(solution)/shard_map/ppermute | solution.py:597
  37.3 1.5 %collective-permute-start.11 = (bf16[16,32,512]{2,1,0:T(8,128)(2,1)}, bf16[16,32,512]{2,1,0:T(8,128)(2,1)S(1)}, u32[]{:S(2)}, u32[]{:S(2)}) collective-permute-start(bf16[16,32,512]{2,1,0:T(8,128)(2,1)} %get-tuple-element.91), channel_id=1, source_target_pairs={{0,24},{4,28},{8,16},{12,20},{16,8},{20,12},{24,0},{28,4},{1,25},{... | collective-permute-start | bytes 1572872 | tf_op jit(solution)/shard_map/ppermute | solution.py:597
  38.8 5.4 %mix.1 = (f32[3,13,512]{2,1,0:T(8,128)}, f32[3,13,512]{2,1,0:T(8,128)}, f32[16,512]{1,0:T(8,128)}, f32[16,512]{1,0:T(8,128)}, f32[16,8]{1,0:T(8,128)}, /*index=5*/bf16[512,32]{1,0:T(8,128)(2,1)}, f32[32,256]{1,0:T(8,128)}) custom-call(bf16[3,13,512]{2,1,0:T(8,128)(2,1)} %bitcast.34, bf16[3,13,512]{2,1,0:T(8,128)(2,1)} %bitcast.35, bf16[4,512]{1,0:T(4,128)(2,1)} %cw_x.1, ...), custom_call_target="tpu_custom_call" | custom-call | flops 1 | bytes 1 | tf_op jit(solution)/shard_map/mix/pallas_call | solution.py:718
  44.8 3.1 %output.1 = bf16[64,512]{1,0:T(8,128)(2,1)} custom-call(f32[16,512]{1,0:T(8,128)} %get-tuple-element.73.gated, bf16[512,2048]{1,0:T(8,128)(2,1)} %w_ssm.1, bf16[256,2048]{1,0:T(8,128)(2,1)} %w_attn.1, f32[64,384]{1,0:T(8,128)} %bitcast.30), custom_call_target="tpu_custom_call" | custom-call | flops 1 | bytes 1 | tf_op jit(solution)/shard_map/output/pallas_call | solution.py:742
  49.4 1.6 %collective-permute-start.12 = (bf16[16,32,512]{2,1,0:T(8,128)(2,1)}, bf16[16,32,512]{2,1,0:T(8,128)(2,1)S(1)}, u32[]{:S(2)}, u32[]{:S(2)}) collective-permute-start(bf16[16,32,512]{2,1,0:T(8,128)(2,1)} %get-tuple-element.93), channel_id=1, source_target_pairs={{0,28},{4,24},{8,20},{12,16},{16,12},{20,8},{24,4},{28,0},{1,29},{... | collective-permute-start | bytes 1572872 | tf_op jit(solution)/shard_map/ppermute | solution.py:597
  51.0 10.9 %all_to_all.33 = bf16[4,16,512]{2,1,0:T(8,128)(2,1)} all-to-all(bf16[4,16,512]{2,1,0:T(8,128)(2,1)} %bitcast.31), channel_id=1, replica_groups=mesh['rows'=8,'cols'=4] {'cols'}, dimensions={0} | all-to-all | bytes 131072 | tf_op jit(solution)/shard_map/all_to_all | solution.py:593
  61.9 1.7 %total.1 = bf16[128,512]{1,0:T(8,128)(2,1)} custom-call(s32[47]{0:T(128)} %get-tuple-element.52.plan, f32[16,512]{1,0:T(8,128)} %get-tuple-element.78.kv_new, f32[16,512]{1,0:T(8,128)} %get-tuple-element.79.driven, f32[16,8]{1,0:T(8,128)} %get-tuple-element.75.decay, f32[32,256]{1,0:T(8,128)} %get-tuple-element.76.b_twice, ...), custom_call_target="tpu_custom_call" | custom-call | flops 1 | bytes 1 | tf_op jit(solution)/shard_map/total/pallas_call | solution.py:771
  63.6 3.4 %all-to-all-start.2 = ((bf16[8,16,512]{2,1,0:T(8,128)(2,1)}), bf16[8,16,512]{2,1,0:T(8,128)(2,1)S(1)}, u32[]{:S(2)}, u32[]{:S(2)}) async-start(bf16[8,16,512]{2,1,0:T(8,128)(2,1)} %bitcast.29), calls=%async_computation.2 | async-start | bytes 262144 | tf_op jit(solution)/shard_map/all_to_all | solution.py:593
  67.1 5.2 %stay.1.state_in = bf16[13,8,64,256]{3,2,1,0:T(8,128)(2,1)} custom-call(s32[47]{0:T(128)} %get-tuple-element.52.plan, bf16[512,32]{1,0:T(8,128)(2,1)} %get-tuple-element.74.drive, f32[16,8]{1,0:T(8,128)} %get-tuple-element.75.decay, f32[32,256]{1,0:T(8,128)} %get-tuple-element.76.b_twice, bf16[13,8,64,256]{3,2,1,0:T(8,128)(2,1)} %state.5), custom_call_target="tpu_custom_call" | custom-call | flops 1 | bytes 1 | tf_op jit(solution)/shard_map/stay/pallas_call | solution.py:754
  72.3 1.6 %all-to-all-done.2 = bf16[8,16,512]{2,1,0:T(8,128)(2,1)S(1)} async-done(((bf16[8,16,512]{2,1,0:T(8,128)(2,1)}), bf16[8,16,512]{2,1,0:T(8,128)(2,1)S(1)}, u32[]{:S(2)}, u32[]{:S(2)}) %all-to-all-start.2) | async-done | bytes 131104 | tf_op jit(solution)/shard_map/all_to_all | solution.py:593
  74.0 0.9 %copy-done.3 = bf16[8,32,512]{2,1,0:T(8,128)(2,1)S(1)} copy-done((bf16[8,32,512]{2,1,0:T(8,128)(2,1)S(1)}, bf16[8,32,512]{2,1,0:T(8,128)(2,1)}, u32[]{:S(2)}) %copy-start.3) | copy-done | bytes 262168
  74.9 0.9 %copy-done.5 = bf16[8,32,512]{2,1,0:T(8,128)(2,1)S(1)} copy-done((bf16[8,32,512]{2,1,0:T(8,128)(2,1)S(1)}, bf16[8,32,512]{2,1,0:T(8,128)(2,1)}, u32[]{:S(2)}) %copy-start.5) | copy-done | bytes 262168
  75.9 4.0 %arrive.1 = (bf16[13,512]{1,0:T(8,128)(2,1)}, bf16[3,13,512]{2,1,0:T(8,128)(2,1)}, bf16[3,13,512]{2,1,0:T(8,128)(2,1)}, bf16[13,8,64,256]{3,2,1,0:T(8,128)(2,1)}, bf16[104,32,512]{2,1,0:T(8,128)(2,1)}) custom-call(s32[1]{0:T(128)} %bitcast.col_ref, s32[47]{0:T(128)S(1)} %copy-done.7, ...), custom_call_target="tpu_custom_call", output_to_operand_aliasing={{3}: (5, {}), {4}: (6, {})} | custom-call | flops 1 | bytes 1 | tf_op jit(solution)/shard_map/arrive/pallas_call | solution.py:783
  (41 shorter events, 5.7 us)
Async XLA Ops:
  6.3 4.6 %collective-permute-start = (bf16[64,3328]{1,0:T(8,128)(2,1)}, bf16[64,3328]{1,0:T(8,128)(2,1)S(1)}, u32[]{:S(2)}, u32[]{:S(2)}) collective-permute-start(bf16[64,3328]{1,0:T(8,128)(2,1)} %get-tuple-element.54), channel_id=1, source_target_pairs={{0,4},{4,0},{8,12},{12,8},{16,20},{20,16},{24,28},{28,24},{1,5},{5... | collective-permute-start | bytes 1277960 | tf_op jit(solution)/shard_map/ppermute | solution.py:597
  6.8 10.5 %collective-permute-start.4 = (bf16[8,32,512]{2,1,0:T(8,128)(2,1)}, bf16[8,32,512]{2,1,0:T(8,128)(2,1)S(1)}, u32[]{:S(2)}, u32[]{:S(2)}) collective-permute-start(bf16[8,32,512]{2,1,0:T(8,128)(2,1)} %get-tuple-element.59), channel_id=1, source_target_pairs={{0,8},{4,12},{8,0},{12,4},{16,24},{20,28},{24,16},{28,20},{1,9},{5... | collective-permute-start | bytes 786440 | tf_op jit(solution)/shard_map/ppermute | solution.py:597
  9.4 9.4 %collective-permute-start.5 = (bf16[8,32,512]{2,1,0:T(8,128)(2,1)}, bf16[8,32,512]{2,1,0:T(8,128)(2,1)S(1)}, u32[]{:S(2)}, u32[]{:S(2)}) collective-permute-start(bf16[8,32,512]{2,1,0:T(8,128)(2,1)} %get-tuple-element.60), channel_id=1, source_target_pairs={{0,16},{4,20},{8,24},{12,28},{16,0},{20,4},{24,8},{28,12},{1,17},{... | collective-permute-start | bytes 786440 | tf_op jit(solution)/shard_map/ppermute | solution.py:597
  13.8 5.9 %collective-permute-start.1 = (bf16[16,3328]{1,0:T(8,128)(2,1)}, bf16[16,3328]{1,0:T(8,128)(2,1)S(1)}, u32[]{:S(2)}, u32[]{:S(2)}) collective-permute-start(bf16[16,3328]{1,0:T(8,128)(2,1)} %get-tuple-element.56), channel_id=1, source_target_pairs={{0,8},{4,12},{8,0},{12,4},{16,24},{20,28},{24,16},{28,20},{1,9},{5... | collective-permute-start | bytes 319496 | tf_op jit(solution)/shard_map/ppermute | solution.py:597
  14.3 8.3 %collective-permute-start.2 = (bf16[16,3328]{1,0:T(8,128)(2,1)}, bf16[16,3328]{1,0:T(8,128)(2,1)S(1)}, u32[]{:S(2)}, u32[]{:S(2)}) collective-permute-start(bf16[16,3328]{1,0:T(8,128)(2,1)} %get-tuple-element.57), channel_id=1, source_target_pairs={{0,16},{4,20},{8,24},{12,28},{16,0},{20,4},{24,8},{28,12},{1,17},{... | collective-permute-start | bytes 319496 | tf_op jit(solution)/shard_map/ppermute | solution.py:597
  15.7 6.9 %collective-permute-start.3 = (bf16[16,3328]{1,0:T(8,128)(2,1)}, bf16[16,3328]{1,0:T(8,128)(2,1)S(1)}, u32[]{:S(2)}, u32[]{:S(2)}) collective-permute-start(bf16[16,3328]{1,0:T(8,128)(2,1)} %get-tuple-element.58), channel_id=1, source_target_pairs={{0,24},{4,28},{8,16},{12,20},{16,8},{20,12},{24,0},{28,4},{1,25},{... | collective-permute-start | bytes 319496 | tf_op jit(solution)/shard_map/ppermute | solution.py:597
  19.7 5.0 %copy-start.9 = (bf16[16,3328]{1,0:T(8,128)(2,1)}, bf16[16,3328]{1,0:T(8,128)(2,1)S(1)}, u32[]{:S(2)}) copy-start(bf16[16,3328]{1,0:T(8,128)(2,1)S(1)} %collective-permute-done.1.rest_1_) | copy-start | bytes 319492
  22.6 2.1 %copy-start.10 = (bf16[16,3328]{1,0:T(8,128)(2,1)}, bf16[16,3328]{1,0:T(8,128)(2,1)S(1)}, u32[]{:S(2)}) copy-start(bf16[16,3328]{1,0:T(8,128)(2,1)S(1)} %collective-permute-done.2.rest_2_) | copy-start | bytes 319492
  22.6 2.1 %copy-start.11 = (bf16[16,3328]{1,0:T(8,128)(2,1)}, bf16[16,3328]{1,0:T(8,128)(2,1)S(1)}, u32[]{:S(2)}) copy-start(bf16[16,3328]{1,0:T(8,128)(2,1)S(1)} %collective-permute-done.3.rest_3_) | copy-start | bytes 319492
  22.6 25.4 %collective-permute-start.7 = (bf16[8,32,512]{2,1,0:T(8,128)(2,1)}, bf16[8,32,512]{2,1,0:T(8,128)(2,1)S(1)}, u32[]{:S(2)}, u32[]{:S(2)}) collective-permute-start(bf16[8,32,512]{2,1,0:T(8,128)(2,1)} %get-tuple-element.83), channel_id=1, source_target_pairs={{0,8},{4,12},{8,0},{12,4},{16,24},{20,28},{24,16},{28,20},{1,9},{5... | collective-permute-start | bytes 786440 | tf_op jit(solution)/shard_map/ppermute | solution.py:597
  23.8 24.9 %collective-permute-start.9 = (bf16[8,32,512]{2,1,0:T(8,128)(2,1)}, bf16[8,32,512]{2,1,0:T(8,128)(2,1)S(1)}, u32[]{:S(2)}, u32[]{:S(2)}) collective-permute-start(bf16[8,32,512]{2,1,0:T(8,128)(2,1)} %get-tuple-element.87), channel_id=1, source_target_pairs={{0,16},{4,20},{8,24},{12,28},{16,0},{20,4},{24,8},{28,12},{1,17},{... | collective-permute-start | bytes 786440 | tf_op jit(solution)/shard_map/ppermute | solution.py:597
  30.7 13.5 %all-to-all-start = ((f32[4,16,384]{2,1,0:T(8,128)}), f32[4,16,384]{2,1,0:T(8,128)S(1)}, u32[]{:S(2)}, u32[]{:S(2)}) async-start(f32[4,16,384]{2,1,0:T(8,128)} %bitcast.33), calls=%async_computation | async-start | bytes 196608 | tf_op jit(solution)/shard_map/all_to_all | solution.py:593
  35.6 38.3 %collective-permute-start.8 = (bf16[16,32,512]{2,1,0:T(8,128)(2,1)}, bf16[16,32,512]{2,1,0:T(8,128)(2,1)S(1)}, u32[]{:S(2)}, u32[]{:S(2)}) collective-permute-start(bf16[16,32,512]{2,1,0:T(8,128)(2,1)} %get-tuple-element.85), channel_id=1, source_target_pairs={{0,12},{4,8},{8,4},{12,0},{16,28},{20,24},{24,20},{28,16},{1,13},{... | collective-permute-start | bytes 1572872 | tf_op jit(solution)/shard_map/ppermute | solution.py:597
  35.6 38.3 %collective-permute-start.10 = (bf16[16,32,512]{2,1,0:T(8,128)(2,1)}, bf16[16,32,512]{2,1,0:T(8,128)(2,1)S(1)}, u32[]{:S(2)}, u32[]{:S(2)}) collective-permute-start(bf16[16,32,512]{2,1,0:T(8,128)(2,1)} %get-tuple-element.89), channel_id=1, source_target_pairs={{0,20},{4,16},{8,28},{12,24},{16,4},{20,0},{24,12},{28,8},{1,21},{... | collective-permute-start | bytes 1572872 | tf_op jit(solution)/shard_map/ppermute | solution.py:597
  37.3 36.6 %collective-permute-start.11 = (bf16[16,32,512]{2,1,0:T(8,128)(2,1)}, bf16[16,32,512]{2,1,0:T(8,128)(2,1)S(1)}, u32[]{:S(2)}, u32[]{:S(2)}) collective-permute-start(bf16[16,32,512]{2,1,0:T(8,128)(2,1)} %get-tuple-element.91), channel_id=1, source_target_pairs={{0,24},{4,28},{8,16},{12,20},{16,8},{20,12},{24,0},{28,4},{1,25},{... | collective-permute-start | bytes 1572872 | tf_op jit(solution)/shard_map/ppermute | solution.py:597
  48.7 25.2 %collective-permute-start.6 = (bf16[16,32,512]{2,1,0:T(8,128)(2,1)}, bf16[16,32,512]{2,1,0:T(8,128)(2,1)S(1)}, u32[]{:S(2)}, u32[]{:S(2)}) collective-permute-start(bf16[16,32,512]{2,1,0:T(8,128)(2,1)} %get-tuple-element.81), channel_id=1, source_target_pairs={{0,4},{4,0},{8,12},{12,8},{16,20},{20,16},{24,28},{28,24},{1,5},{5... | collective-permute-start | bytes 1572872 | tf_op jit(solution)/shard_map/ppermute | solution.py:597
  49.4 24.5 %collective-permute-start.12 = (bf16[16,32,512]{2,1,0:T(8,128)(2,1)}, bf16[16,32,512]{2,1,0:T(8,128)(2,1)S(1)}, u32[]{:S(2)}, u32[]{:S(2)}) collective-permute-start(bf16[16,32,512]{2,1,0:T(8,128)(2,1)} %get-tuple-element.93), channel_id=1, source_target_pairs={{0,28},{4,24},{8,20},{12,16},{16,12},{20,8},{24,4},{28,0},{1,29},{... | collective-permute-start | bytes 1572872 | tf_op jit(solution)/shard_map/ppermute | solution.py:597
  63.6 10.3 %all-to-all-start.2 = ((bf16[8,16,512]{2,1,0:T(8,128)(2,1)}), bf16[8,16,512]{2,1,0:T(8,128)(2,1)S(1)}, u32[]{:S(2)}, u32[]{:S(2)}) async-start(bf16[8,16,512]{2,1,0:T(8,128)(2,1)} %bitcast.29), calls=%async_computation.2 | async-start | bytes 262144 | tf_op jit(solution)/shard_map/all_to_all | solution.py:593
  67.0 6.9 %copy-start = (f32[3,13,512]{2,1,0:T(8,128)S(1)}, f32[3,13,512]{2,1,0:T(8,128)}, u32[]{:S(2)}) copy-start(f32[3,13,512]{2,1,0:T(8,128)} %get-tuple-element.70.conv_x) | copy-start | bytes 239620
  67.0 6.9 %copy-start.1 = (f32[3,13,512]{2,1,0:T(8,128)S(1)}, f32[3,13,512]{2,1,0:T(8,128)}, u32[]{:S(2)}) copy-start(f32[3,13,512]{2,1,0:T(8,128)} %get-tuple-element.71.conv_bc) | copy-start | bytes 239620
  67.0 6.9 %copy-start.6 = (s32[1,1,13,8]{2,3,1,0:T(8,128)S(1)}, s32[1,1,13,8]{2,3,1,0:T(8,128)}, u32[]{:S(2)}) copy-start(s32[1,1,13,8]{2,3,1,0:T(8,128)} %param.28) | copy-start | bytes 1252
  67.1 6.9 %copy-start.7 = (s32[47]{0:T(128)S(1)}, s32[47]{0:T(128)}, u32[]{:S(2)}) copy-start(s32[47]{0:T(128)} %get-tuple-element.52.plan) | copy-start | bytes 568
  74.0 1.0 %copy-start.3 = (bf16[8,32,512]{2,1,0:T(8,128)(2,1)S(1)}, bf16[8,32,512]{2,1,0:T(8,128)(2,1)}, u32[]{:S(2)}) copy-start(bf16[8,32,512]{2,1,0:T(8,128)(2,1)} %copy-done.2) | copy-start | bytes 786436
  74.9 0.9 %copy-start.5 = (bf16[8,32,512]{2,1,0:T(8,128)(2,1)S(1)}, bf16[8,32,512]{2,1,0:T(8,128)(2,1)}, u32[]{:S(2)}) copy-start(bf16[8,32,512]{2,1,0:T(8,128)(2,1)} %copy-done.4) | copy-start | bytes 786436
  (4 other events, 2.8 us)
